TPU v7x, 256 devices: a whole 4x4x8 slice. The times are simulated.
256 devices in a mesh: seq: 16 (over y, x), exp: 16 (over z, core).
Axes of the slice: x: 4, y: 4, z: 8, core: 2. Of those that a mesh axis runs over, the one named last changes fastest.
Arguments:
- enc_in: bfloat16 [16, 4096, 1024], P('exp', 'seq'), may hold values from -6 to 6
- expert_ids: int32 [16, 4096], P('exp', 'seq'), may hold values from 0 to 63, as said below
- slots: int32 [16, 4096], P('exp', 'seq'), may hold values from 0 to 4, as said below
- expert_gate: float32 [16, 4096], P('exp', 'seq'), may hold values from 0.2 to 1
- moe_gain: float32 [1024], replicated, may hold values from 0.25 to 1.75
- w_in: bfloat16 [64, 1024, 2816], P('exp', None, 'seq'), may hold values from -0.1875 to 0.1875
- w_out: bfloat16 [64, 2816, 1024], P('exp', 'seq'), may hold values from -0.109375 to 0.109375
- final_gain: float32 [1024], replicated, may hold values from 0.25 to 1.75
- w_key: bfloat16 [1024, 1024], replicated, may hold values from -0.1875 to 0.1875
- w_value: bfloat16 [1024, 1024], replicated, may hold values from -0.1875 to 0.1875
- dec_query: bfloat16 [16, 2048, 1024], P('exp', 'seq'), may hold values from -400 to 400
Outputs:
- enc_out: bfloat16 [16, 4096, 1024], P('exp', 'seq')
- context: bfloat16 [16, 2048, 1024], P('exp', 'seq')
Inputs may be any that keep to these rules, and one draw needn't show every extreme that they name: `expert_ids`: in every device block of 256 consecutive tokens of a document, some expert is named by more than 4 tokens. slots of a token is the number of earlier tokens of its device block of 256 tokens that name the same expert, or 4 if that number is 4 or more (the token is dropped).
All inputs are finite; a program needn't handle non-finite values.
Results may differ from a plain program's by a relative error of at most 0.039.
Values may be sent and summed in bfloat16 or wider, within the bound.
A program may use at most 128 MiB of HBM per device.

v0:
```python
import jax
import jax.numpy as jnp
from jax import lax
from jax.sharding import PartitionSpec as P

HEADS = 16


def rms_scale(values, gain):
    mean_square = jnp.mean(values * values, axis=-1, keepdims=True)
    return values * lax.rsqrt(mean_square + 1e-06) * gain


def per_device(
    enc_in,
    expert_ids,
    slots,
    expert_gate,
    moe_gain,
    w_in,
    w_out,
    final_gain,
    w_key,
    w_value,
    dec_query,
):
    n_exp = lax.axis_size("exp")
    tok_rows = enc_in.shape[1]
    width = enc_in.shape[2]
    exp_local = w_in.shape[0]
    capacity = tok_rows // (exp_local * n_exp)
    inputs = enc_in[0].astype(jnp.float32)
    normed = rms_scale(inputs, moe_gain).astype(jnp.bfloat16)
    route = expert_ids[0]
    slot_pos = slots[0]
    kept = slot_pos < capacity
    target = route // exp_local * (capacity * exp_local) + slot_pos * exp_local + route % exp_local
    target = jnp.where(kept, target, -1)
    places = jnp.arange(tok_rows, dtype=jnp.int32)
    dispatch = (places[:, None] == target[None, :]).astype(jnp.bfloat16)
    combine = (target[:, None] == places[None, :]).astype(jnp.bfloat16)
    packed = jnp.dot(dispatch, normed, preferred_element_type=jnp.float32).astype(jnp.bfloat16)
    packed = packed.reshape(n_exp, capacity, exp_local, width)
    arrived = lax.all_to_all(packed, "exp", split_axis=0, concat_axis=0, tiled=True)
    arrived = arrived.reshape(n_exp * capacity, exp_local, width)
    product = jnp.einsum(
        "red,edf->ref",
        lax.all_gather(arrived, "seq", axis=0, tiled=True),
        w_in,
        preferred_element_type=jnp.float32,
    )
    hidden = jnp.maximum(product, 0.0).astype(jnp.bfloat16)
    summed = lax.psum_scatter(
        jnp.einsum("ref,efd->red", hidden, w_out, preferred_element_type=jnp.float32),
        "seq",
        scatter_dimension=0,
        tiled=True,
    )
    result = summed.astype(jnp.bfloat16).reshape(n_exp, capacity, exp_local, width)
    back = lax.all_to_all(result, "exp", split_axis=0, concat_axis=0, tiled=True).reshape(
        tok_rows, width
    )
    combined = jnp.dot(combine, back, preferred_element_type=jnp.float32)
    enc_rows = inputs + expert_gate[0][:, None] * combined
    enc_out = enc_rows.astype(jnp.bfloat16)
    kv_rows = rms_scale(enc_out.astype(jnp.float32), final_gain).astype(jnp.bfloat16)
    head_dim = width // HEADS
    factor = head_dim ** (-0.5)
    query = dec_query[0]
    q_count = query.shape[0]
    q_heads = query.reshape(q_count, HEADS, head_dim)
    keys = jnp.dot(kv_rows, w_key, preferred_element_type=jnp.float32).astype(jnp.bfloat16)
    values = jnp.dot(kv_rows, w_value, preferred_element_type=jnp.float32).astype(jnp.bfloat16)
    fold_keys = lax.all_gather(keys, "seq", axis=0, tiled=True)
    fold_values = lax.all_gather(values, "seq", axis=0, tiled=True)
    running_max = jnp.full((HEADS, q_count), -1e30, jnp.float32)
    k_heads = fold_keys.reshape(fold_keys.shape[0], HEADS, head_dim)
    v_heads = fold_values.reshape(fold_values.shape[0], HEADS, head_dim)
    scores = (
        jnp.einsum("qhd,khd->hqk", q_heads, k_heads, preferred_element_type=jnp.float32) * factor
    )
    new_max = jnp.maximum(running_max, jnp.max(scores, axis=-1))
    expo = jnp.exp(scores - new_max[:, :, None])
    new_sum = jnp.sum(expo, axis=-1)
    update = jnp.einsum(
        "hqk,khd->qhd", expo.astype(jnp.bfloat16), v_heads, preferred_element_type=jnp.float32
    )
    attended = update / jnp.transpose(new_sum)[:, :, None]
    context = attended.reshape(q_count, width).astype(jnp.bfloat16)
    return (enc_out[None], context[None])


def solution(mesh):
    placed = (
        P("exp", "seq", None),
        P("exp", "seq"),
        P("exp", "seq"),
        P("exp", "seq"),
        P(),
        P("exp", None, "seq"),
        P("exp", "seq", None),
        P(),
        P(),
        P(),
        P("exp", "seq", None),
    )
    return jax.shard_map(
        per_device,
        mesh=mesh,
        in_specs=placed,
        out_specs=(P("exp", "seq", None), P("exp", "seq", None)),
        check_vma=False,
    )
```

profile of v0, /device:TPU:2, one launch (start us, length us, event | category | flops | bytes accessed | tf_op | source)
XLA Modules:
  0.0 459.5 jit_solution(15930327528415837515)
XLA Ops:
  7.2 0.0 all-gather.4.cloned.1.call-start
  7.2 1.4 fusion.21
  8.6 0.7 broadcast_multiply_fusion
  9.3 1.5 convolution_convert_fusion.2
  10.8 0.2 reshape.124
  11.0 24.5 %all_to_all.10 = bf16[16,4,4,1024]{3,2,1,0:T(4,128)(2,1)} all-to-all(bf16[16,4,4,1024]{3,2,1,0:T(4,128)(2,1)S(1)} %reshape.124), channel_id=1, replica_groups=mesh['seq'=16,'exp'=16] {'exp'}, dimensions={0} | all-to-all | bytes 1048576 | tf_op jit(solution)/shard_map/all_to_all | solution.py:44
  35.5 0.0 all-gather.4.cloned.1.call-update
  35.5 0.0 reduce-scatter.2.cloned.1.call-start
  35.6 74.4 %all-gather.4.cloned.1.call-done = bf16[1024,4,1024]{2,1,0:T(4,128)(2,1)} async-done(((bf16[64,4,1024]{2,1,0:T(4,128)(2,1)}), bf16[1024,4,1024]{2,1,0:T(4,128)(2,1)}) %all-gather.4.cloned.1.call-update) | async-done | bytes 8388624 | tf_op jit(solution)/shard_map/all_gather | solution.py:48
  110.0 17.6 %convolution_bitcast_fusion = f32[1024,4,1024]{2,0,1:T(8,128)} fusion(bf16[4,176,1024]{2,1,0:T(8,128)(2,1)} %param.17, bf16[4,1024,176]{1,2,0:T(8,128)(2,1)} %param.16, bf16[1024,4,1024]{2,1,0:T(4,128)(2,1)} %all-gather.4.cloned.1.call-done), kind=kOutput, calls=%fused_computation.8 | convolution fusion | flops 2954231808 | bytes 28049408 | tf_op jit(solution)/shard_map/ref,efd->red/dot_general | solution.py:54
  127.7 0.0 reduce-scatter.2.cloned.1.call-update
  127.7 115.3 %reduce-scatter.2.cloned.1.call-done = f32[64,4,1024]{2,0,1:T(8,128)} async-done(((f32[1024,4,1024]{2,0,1:T(8,128)}), f32[64,4,1024]{2,0,1:T(8,128)}) %reduce-scatter.2.cloned.1.call-update) | async-done | bytes 1048592 | tf_op jit(solution)/shard_map/reduce_scatter | solution.py:53
  243.0 1.3 convert_element_type.60
  244.3 1.2 copy.32
  245.5 7.1 %all-to-all-start.1 = ((bf16[16,4,4,1024]{3,2,1,0:T(4,128)(2,1)}), bf16[16,4,4,1024]{3,2,1,0:T(4,128)(2,1)S(1)}, u32[]{:S(2)}, u32[]{:S(2)}) async-start(bf16[16,4,4,1024]{3,2,1,0:T(4,128)(2,1)} %bitcast.9), calls=%async_computation.2 | async-start | bytes 1048576 | tf_op jit(solution)/shard_map/all_to_all | solution.py:60
  252.6 0.0 all-gather.8.cloned.1.call-start
  252.7 15.9 %all-to-all-done.1 = bf16[16,4,4,1024]{3,2,1,0:T(4,128)(2,1)S(1)} async-done(((bf16[16,4,4,1024]{3,2,1,0:T(4,128)(2,1)}), bf16[16,4,4,1024]{3,2,1,0:T(4,128)(2,1)S(1)}, u32[]{:S(2)}, u32[]{:S(2)}) %all-to-all-start.1) | async-done | bytes 524320 | tf_op jit(solution)/shard_map/all_to_all | solution.py:60
  268.6 0.9 reshape.127
  269.6 1.5 fusion.18
  271.1 0.8 copy-done.8
  271.9 1.6 convolution_convert_fusion
  273.5 0.2 all-gather.6.cloned.1.call-start
  273.7 3.3 convolution_convert_fusion.1
  277.1 0.2 copy.28
  277.3 69.1 %all-gather.8.cloned.1.call-done = bf16[4096,1024]{1,0:T(8,128)(2,1)} async-done(((bf16[256,1024]{1,0:T(8,128)(2,1)}), bf16[4096,1024]{1,0:T(8,128)(2,1)}) %all-gather.8.cloned.1.call-update) | async-done | bytes 8388624 | tf_op jit(solution)/shard_map/all_gather | solution.py:74
  346.3 11.7 %copy.27 = bf16[4096,1024]{0,1:T(8,128)(2,1)} copy(bf16[4096,1024]{1,0:T(8,128)(2,1)} %all-gather.8.cloned.1.call-done) | data formatting | bytes 16777216 | tf_op jit(solution)/shard_map/all_gather | solution.py:74
  358.1 16.2 %bitcast_reduce_fusion = (f32[16,128]{1,0:T(8,128)S(1)}, f32[16,4096,128]{2,1,0:T(8,128)}) fusion(bf16[4096,16,64]{0,2,1:T(8,128)(2,1)} %bitcast.63, bf16[128,16,64]{0,2,1:T(8,128)(2,1)S(1)} %bitcast.66), kind=kOutput, calls=%fused_computation.1 | convolution fusion | flops 1090516992 | bytes 42213376 | tf_op jit(solution)/shard_map/qhd,khd->hqk/dot_general | solution.py:80
  374.3 13.5 %fusion.1 = f32[16,128]{1,0:T(8,128)S(1)} fusion(f32[16,4096,128]{2,1,0:T(8,128)} %get-tuple-element.13, f32[16,128]{1,0:T(8,128)S(1)} %broadcast_maximum_fusion), kind=kLoop, calls=%fused_computation.3 | loop fusion | flops 25163776 | bytes 33570816 | tf_op jit(solution)/shard_map/reduce_sum | solution.py:84
  387.8 36.3 %all-gather.6.cloned.1.call-done = bf16[4096,1024]{1,0:T(8,128)(2,1)} async-done(((bf16[256,1024]{1,0:T(8,128)(2,1)}), bf16[4096,1024]{1,0:T(8,128)(2,1)}) %all-gather.6.cloned.1.call-update) | async-done | bytes 8388624 | tf_op jit(solution)/shard_map/all_gather | solution.py:75
  424.1 11.7 %copy.26 = bf16[4096,1024]{0,1:T(8,128)(2,1)} copy(bf16[4096,1024]{1,0:T(8,128)(2,1)} %all-gather.6.cloned.1.call-done) | data formatting | bytes 16777216 | tf_op jit(solution)/shard_map/all_gather | solution.py:75
  435.9 16.2 %fusion.27 = bf16[128,16,64]{0,2,1:T(8,128)(2,1)S(1)} fusion(bf16[4096,16,64]{0,2,1:T(8,128)(2,1)} %bitcast.64, f32[16,4096,128]{2,1,0:T(8,128)} %get-tuple-element.13, f32[16,128]{1,0:T(8,128)S(1)} %broadcast_maximum_fusion, f32[128,16]{0,1:T(8,128)S(1)} %bitcast.68), kind=kOutput, calls=%fused_computation.31 | convolution fusion | flops 1099169792 | bytes 42221568 | tf_op jit(solution)/shard_map/hqk,khd->qhd/dot_general | solution.py:85
  452.1 0.9 copy.30
  (24 shorter events, 0.1 us)
Async XLA Ops:
  7.2 264.7 %copy-start = (bf16[1024,1024]{1,0:T(8,128)(2,1)S(1)}, bf16[1024,1024]{1,0:T(8,128)(2,1)}, u32[]{:S(2)}) copy-start(bf16[1024,1024]{1,0:T(8,128)(2,1)} %param.19) | copy-start | bytes 6291460
  7.2 102.8 %all-gather.4.cloned.1.call-start = ((), (), s32[]{:S(2)}) async-start(), calls=%async_computation.3 | async-start | bytes 8912896 | tf_op jit(solution)/shard_map/all_gather | solution.py:48
  35.5 207.5 %reduce-scatter.2.cloned.1.call-start = ((), (), s32[]{:S(2)}) async-start(), calls=%async_computation.4 | async-start | bytes 17825792 | tf_op jit(solution)/shard_map/reduce_scatter | solution.py:53
  127.6 125.0 %copy-start.5 = (s32[1,256]{1,0:T(1,128)S(1)}, s32[1,256]{1,0:T(1,128)}, u32[]{:S(2)}) copy-start(s32[1,256]{1,0:T(1,128)} %param.13) | copy-start | bytes 3076
  127.6 125.1 %copy-start.4 = (s32[1,256]{1,0:T(1,128)S(1)}, s32[1,256]{1,0:T(1,128)}, u32[]{:S(2)}) copy-start(s32[1,256]{1,0:T(1,128)} %param.12) | copy-start | bytes 3076
  127.6 141.9 %copy-start.2 = (bf16[1,256,1024]{2,1,0:T(8,128)(2,1)S(1)}, bf16[1,256,1024]{2,1,0:T(8,128)(2,1)}, u32[]{:S(2)}) copy-start(bf16[1,256,1024]{2,1,0:T(8,128)(2,1)} %param.11) | copy-start | bytes 1572868
  127.6 141.9 %copy-start.7 = (f32[1,256]{1,0:T(1,128)S(1)}, f32[1,256]{1,0:T(1,128)}, u32[]{:S(2)}) copy-start(f32[1,256]{1,0:T(1,128)} %param.14) | copy-start | bytes 3076
  127.6 144.2 %copy-start.6 = (f32[1024]{0:T(1024)S(1)}, f32[1024]{0:T(1024)}, u32[]{:S(2)}) copy-start(f32[1024]{0:T(1024)} %param.18) | copy-start | bytes 12292
  127.7 149.4 %copy-start.3 = (bf16[1,128,1024]{2,1,0:T(8,128)(2,1)S(1)}, bf16[1,128,1024]{2,1,0:T(8,128)(2,1)}, u32[]{:S(2)}) copy-start(bf16[1,128,1024]{2,1,0:T(8,128)(2,1)} %param.21) | copy-start | bytes 786436
  245.5 23.2 %all-to-all-start.1 = ((bf16[16,4,4,1024]{3,2,1,0:T(4,128)(2,1)}), bf16[16,4,4,1024]{3,2,1,0:T(4,128)(2,1)S(1)}, u32[]{:S(2)}, u32[]{:S(2)}) async-start(bf16[16,4,4,1024]{3,2,1,0:T(4,128)(2,1)} %bitcast.9), calls=%async_computation.2 | async-start | bytes 1048576 | tf_op jit(solution)/shard_map/all_to_all | solution.py:60
  252.6 93.7 %all-gather.8.cloned.1.call-start = ((), (), s32[]{:S(2)}) async-start(), calls=%async_computation.6 | async-start | bytes 8912896 | tf_op jit(solution)/shard_map/all_gather | solution.py:74
  271.1 0.8 copy-start.8
  273.5 150.7 %all-gather.6.cloned.1.call-start = ((), (), s32[]{:S(2)}) async-start(), calls=%async_computation.5 | async-start | bytes 8912896 | tf_op jit(solution)/shard_map/all_gather | solution.py:75
  435.9 17.1 %copy-start.1 = (bf16[1024,1024]{1,0:T(8,128)(2,1)S(1)}, bf16[1024,1024]{1,0:T(8,128)(2,1)}, u32[]{:S(2)}) copy-start(bf16[1024,1024]{1,0:T(8,128)(2,1)} %param.19) | copy-start | bytes 6291460
Sparse Core Ops, SparseCore 0:
  35.6 74.3 all-gather.3
  127.8 115.1 reduce-scatter.1
  273.6 72.6 all-gather.7
  348.6 75.4 all-gather.5
where the time goes:
time: 461 us; the launch traced here: 460 us
  waiting for transfers between devices  311 us (67%)
  matrix products  58 us (13%)
  local copies, waits for them, and re-layouts  27.6 us (6%)
  blocking collectives  24.5 us (5%)
  other arithmetic  17 us (4%)
  between operations  13.9 us (3%)
  starting transfers between devices  7.46 us (2%)
    reduce_scatter x1, waiting for transfers between devices, per_device(): lax.psum_scatter(jnp.einsum('ref,efd->red', hidden, w_out, preferred_elem...  115 us
    all_gather x1, waiting for transfers between devices, per_device(): lax.all_gather(arrived, 'seq', axis=0, tiled=True)  74.4 us
    all_gather x1, waiting for transfers between devices, per_device(): fold_keys = lax.all_gather(keys, 'seq', axis=0, tiled=True)  69.1 us
    all_gather x1, waiting for transfers between devices, per_device(): fold_values = lax.all_gather(values, 'seq', axis=0, tiled=True)  36.3 us
    all_to_all x1, blocking collectives, per_device(): lax.all_to_all(packed, 'exp', split_axis=0, concat_axis=0, tiled=True)  24.5 us
    dot_general x1, matrix products, per_device(): jnp.einsum('ref,efd->red', hidden, w_out, preferred_element_type=jnp.floa...  17.6 us
    dot_general x1, matrix products, per_device(): jnp.einsum('hqk,khd->qhd', expo.astype(jnp.bfloat16), v_heads, preferred_...  16.2 us
    dot_general x1, matrix products, per_device(): jnp.einsum('qhd,khd->hqk', q_heads, k_heads, preferred_element_type=jnp.f...  16.2 us
  transfers between devices with their start and end apart: 5, of which 5 were waited for; matrix products, arithmetic and copies ran while one was open for 10% of the time, Pallas kernels for 0%

commit v1 on v0

v1 whole, which is shorter than its diff:
```python
import functools

import jax
import jax.numpy as jnp
from jax import lax
from jax.experimental import pallas as pl
from jax.experimental.pallas import tpu as pltpu
from jax.sharding import PartitionSpec as P

HEADS = 16
MESH = pl.DeviceIdType.MESH
F32 = jnp.float32
BF16 = jnp.bfloat16


def rms_scale(values, gain):
    mean_square = jnp.mean(values * values, axis=-1, keepdims=True)
    return values * lax.rsqrt(mean_square + 1e-06) * gain


def rows_at(index, count):
    return pl.ds(pl.multiple_of(index * count, count), count)


def greet(axes):
    barrier = pltpu.get_barrier_semaphore()
    total = 0
    for axis in axes:
        n = lax.axis_size(axis)
        me = lax.axis_index(axis)
        total += n - 1

        def signal(d, carry, axis=axis, n=n, me=me):
            pl.semaphore_signal(
                barrier, inc=1, device_id={axis: lax.rem(me + d, n)}, device_id_type=MESH
            )
            return carry

        lax.fori_loop(1, n, signal, 0)
    pl.semaphore_wait(barrier, total)


class Exchange:
    def __init__(self, axis, source, landing, send, recv):
        self.axis, self.source, self.landing = axis, source, landing
        self.send, self.recv = send, recv
        self.n, self.me = lax.axis_size(axis), lax.axis_index(axis)

    def copy(self, d, slot):
        t = lax.rem(self.me + d, self.n)
        return pltpu.make_async_remote_copy(
            src_ref=self.source(t),
            dst_ref=self.landing(slot),
            send_sem=self.send.at[d],
            recv_sem=self.recv.at[d],
            device_id={self.axis: t},
            device_id_type=MESH,
        )

    def start_one(self, d):
        self.copy(d, self.me).start()

    def wait_one(self, d):
        self.copy(d, lax.rem(self.me + self.n - d, self.n)).wait_recv()

    def loop(self, act):
        def body(d, carry):
            act(d)
            return carry

        lax.fori_loop(1, self.n, body, 0)

    def start(self):
        self.loop(self.start_one)

    def arrived(self):
        self.loop(self.wait_one)

    def sent(self):
        self.loop(lambda d: self.copy(d, self.me).wait_send())


def moe_kernel(
    packed_ref,
    win_ref,
    wout_ref,
    q_ref,
    back_ref,
    qland_ref,
    zland,
    rows,
    rland,
    win_land,
    wout_land,
    part,
    pland,
    brows,
    zback,
    bland,
    qsend,
    local_sem,
    z_send,
    z_recv,
    wi_send,
    wi_recv,
    wo_send,
    wo_recv,
    r_send,
    r_recv,
    p_send,
    p_recv,
    b_send,
    b_recv,
    q_send,
    q_recv,
):
    seq, exp = lax.axis_index("seq"), lax.axis_index("exp")
    n_seq = lax.axis_size("seq")
    experts = win_ref.shape[0]
    share = n_seq // experts
    my_y, my_x = seq // share, lax.rem(seq, share)
    zrows = packed_ref.shape[0] // lax.axis_size("exp")
    srows = packed_ref.shape[0] // experts
    greet(("seq", "exp"))

    z_out = Exchange(
        "exp",
        lambda t: packed_ref.at[rows_at(t, zrows)],
        lambda s: zland.at[rows_at(s, zrows)],
        z_send,
        z_recv,
    )
    z_out.start()
    zland[rows_at(exp, zrows), :] = packed_ref[rows_at(exp, zrows), :]

    def weight_copy(d, slot, ref, land, send, recv):
        k = lax.rem(my_y + d, experts)
        return pltpu.make_async_remote_copy(
            src_ref=ref.at[k],
            dst_ref=land.at[slot],
            send_sem=send.at[d],
            recv_sem=recv.at[d],
            device_id={"seq": k * share + my_x},
            device_id_type=MESH,
        )

    weights = ((win_ref, win_land, wi_send, wi_recv), (wout_ref, wout_land, wo_send, wo_recv))
    for d in range(1, experts):
        for each in weights:
            weight_copy(d, my_y, *each).start()
    own = [
        pltpu.make_async_copy(ref.at[my_y], land.at[my_y], local_sem.at[i])
        for i, (ref, land, _, _) in enumerate(weights)
    ]
    for copy in own:
        copy.start()

    lane = lax.broadcasted_iota(jnp.int32, (q_ref.shape[0], 128), 1)
    for p in range(HEADS // 2):
        pair = pltpu.roll(q_ref[:, p * 128 : (p + 1) * 128].astype(F32) * 0.125, 64, 1)
        qsend[2 * p] = jnp.where(lane >= 64, pair, 0.0).astype(BF16)
        qsend[2 * p + 1] = jnp.where(lane < 64, pair, 0.0).astype(BF16)
    q_out = Exchange(
        "seq", lambda t: qsend.at[t], lambda s: qland_ref.at[s], q_send, q_recv
    )
    q_own = pltpu.make_async_copy(qsend.at[seq], qland_ref.at[seq], local_sem.at[2])
    q_own.start()

    total = packed_ref.shape[0]
    capacity = zrows // experts
    out_row = lax.broadcasted_iota(jnp.int32, (total, total), 0)
    in_row = lax.broadcasted_iota(jnp.int32, (total, total), 1)

    def by_expert(r):
        j, k, c = r // zrows, lax.rem(r // capacity, experts), lax.rem(r, capacity)
        return k * srows + j * capacity + c

    forward = (by_expert(in_row) == out_row).astype(BF16)
    inverse = (by_expert(out_row) == in_row).astype(BF16)

    z_out.arrived()
    rows[...] = jnp.dot(forward, zland[...], preferred_element_type=F32).astype(BF16)

    r_out = Exchange(
        "seq",
        lambda t: rows.at[rows_at(t // share, srows)],
        lambda s: rland.at[rows_at(s, srows)],
        r_send,
        r_recv,
    )
    r_out.start()
    q_out.start()
    rland[rows_at(seq, srows), :] = rows[rows_at(my_y, srows), :]
    for copy in own:
        copy.wait()
    for d in range(1, experts):
        slot = lax.rem(my_y + experts - d, experts)
        for each in weights:
            weight_copy(d, slot, *each).wait_recv()
    r_out.arrived()

    tile = 256

    def ffn(m, carry):
        block = rland[rows_at(m, tile), :]
        acc = None
        for h in range(experts):
            product = jnp.dot(block, win_land[h], preferred_element_type=F32)
            hidden = jnp.maximum(product, 0.0).astype(BF16)
            term = jnp.dot(hidden, wout_land[h], preferred_element_type=F32)
            acc = term if acc is None else acc + term
        part[rows_at(m, tile), :] = acc
        return carry

    lax.fori_loop(0, rland.shape[0] // tile, ffn, 0)

    p_out = Exchange(
        "seq",
        lambda t: part.at[rows_at(t, srows)],
        lambda s: pland.at[s],
        p_send,
        p_recv,
    )
    p_out.start()
    pland[seq] = part[rows_at(seq, srows), :]
    p_out.arrived()
    for k in range(experts):
        acc = pland[k * share]
        for i in range(1, share):
            acc = acc + pland[k * share + i]
        brows[k * srows : (k + 1) * srows, :] = acc.astype(BF16)
    zback[...] = jnp.dot(inverse, brows[...], preferred_element_type=F32).astype(BF16)

    b_out = Exchange(
        "exp",
        lambda t: zback.at[rows_at(t, zrows)],
        lambda s: bland.at[rows_at(s, zrows)],
        b_send,
        b_recv,
    )
    b_out.start()
    bland[rows_at(exp, zrows), :] = zback[rows_at(exp, zrows), :]
    q_own.wait()
    q_out.arrived()
    b_out.arrived()
    back_ref[...] = bland[...]
    for exchange in (z_out, r_out, q_out, p_out, b_out):
        exchange.sent()
    for d in range(1, experts):
        for each in weights:
            weight_copy(d, my_y, *each).wait_send()


def attend_kernel(
    rows_ref,
    wk_ref,
    wv_ref,
    q_ref,
    out_ref,
    kvsend,
    kvland,
    csend,
    cland,
    k_send,
    k_recv,
    c_send,
    c_recv,
):
    seq = lax.axis_index("seq")
    n_seq = lax.axis_size("seq")
    count = rows_ref.shape[0]
    greet(("seq",))
    lane = lax.broadcasted_iota(jnp.int32, (count, 128), 1)
    low = lane < 64
    block = rows_ref[...]
    for g in range(HEADS // 4):
        cols = slice(g * 256, (g + 1) * 256)
        keys = jnp.dot(block, wk_ref[:, cols], preferred_element_type=F32)
        values = jnp.dot(block, wv_ref[:, cols], preferred_element_type=F32)
        for i in range(2):
            k_pair = pltpu.roll(keys[:, i * 128 : (i + 1) * 128], 64, 1)
            v_pair = values[:, i * 128 : (i + 1) * 128]
            head = g * 4 + i * 2
            kvsend[head] = jnp.where(low, v_pair, k_pair).astype(BF16)
            kvsend[head + 1] = jnp.where(low, k_pair, v_pair).astype(BF16)
    kv_out = Exchange(
        "seq",
        lambda t: kvsend.at[t],
        lambda s: kvland.at[rows_at(s, count)],
        k_send,
        k_recv,
    )
    kv_out.start()
    kvland[rows_at(seq, count), :] = kvsend[seq]
    kv_out.arrived()

    c_out = Exchange("seq", lambda t: csend.at[t], lambda s: cland.at[s], c_send, c_recv)

    def attend(t):
        kv = kvland[...]
        scores = lax.dot_general(
            q_ref[t], kv, (((1,), (1,)), ((), ())), preferred_element_type=F32
        )
        expo = jnp.exp(scores - jnp.max(scores, axis=-1, keepdims=True))
        total = jnp.sum(expo, axis=-1, keepdims=True)
        mixed = jnp.dot(expo.astype(BF16), kv, preferred_element_type=F32)
        return (mixed / total).astype(BF16)

    def step(d, carry):
        t = lax.rem(seq + d, n_seq)
        csend[t] = attend(t)
        c_out.start_one(d)
        return carry

    lax.fori_loop(1, n_seq, step, 0)
    cland[seq] = attend(seq)
    c_out.arrived()
    low = lax.broadcasted_iota(jnp.int32, cland.shape[1:], 1) < 64
    for p in range(HEADS // 2):
        out_ref[:, p * 128 : (p + 1) * 128] = jnp.where(low, cland[2 * p], cland[2 * p + 1])
    kv_out.sent()
    c_out.sent()


def per_device(
    enc_in,
    expert_ids,
    slots,
    expert_gate,
    moe_gain,
    w_in,
    w_out,
    final_gain,
    w_key,
    w_value,
    dec_query,
):
    n_exp, n_seq = lax.axis_size("exp"), lax.axis_size("seq")
    tok_rows, width = enc_in.shape[1:]
    experts, _, part_ff = w_in.shape
    capacity = tok_rows // (experts * n_exp)
    srows = tok_rows // experts
    q_rows = dec_query.shape[1]
    inputs = enc_in[0].astype(F32)
    normed = rms_scale(inputs, moe_gain).astype(BF16)
    kept = slots[0] < capacity
    target = jnp.where(kept, expert_ids[0] * capacity + slots[0], -1)
    places = jnp.arange(tok_rows, dtype=jnp.int32)
    dispatch = (places[:, None] == target[None, :]).astype(BF16)
    combine = (target[:, None] == places[None, :]).astype(BF16)
    packed = jnp.dot(dispatch, normed, preferred_element_type=F32).astype(BF16)

    vmem = pl.BlockSpec(memory_space=pltpu.VMEM)
    hbm = pl.BlockSpec(memory_space=pl.ANY)
    dma = pltpu.SemaphoreType.DMA
    back, queries = pl.pallas_call(
        moe_kernel,
        out_shape=(
            jax.ShapeDtypeStruct((tok_rows, width), BF16),
            jax.ShapeDtypeStruct((n_seq, q_rows, 128), BF16),
        ),
        in_specs=[vmem, hbm, hbm, vmem],
        out_specs=(vmem, hbm),
        scratch_shapes=[
            pltpu.VMEM((tok_rows, width), BF16),
            pltpu.VMEM((tok_rows, width), BF16),
            pltpu.VMEM((n_seq * srows, width), BF16),
            pltpu.VMEM((experts, width, part_ff), BF16),
            pltpu.VMEM((experts, part_ff, width), BF16),
            pltpu.VMEM((n_seq * srows, width), F32),
            pltpu.VMEM((n_seq, srows, width), F32),
            pltpu.VMEM((tok_rows, width), BF16),
            pltpu.VMEM((tok_rows, width), BF16),
            pltpu.VMEM((tok_rows, width), BF16),
            pltpu.VMEM((n_seq, q_rows, 128), BF16),
            dma((3,)),
            dma((n_exp,)),
            dma((n_exp,)),
            dma((experts,)),
            dma((experts,)),
            dma((experts,)),
            dma((experts,)),
        ]
        + [dma((n_seq,))] * 4
        + [dma((n_exp,))] * 2
        + [dma((n_seq,))] * 2,
        compiler_params=pltpu.CompilerParams(
            collective_id=0, has_side_effects=True, vmem_limit_bytes=40 << 20
        ),
        name="experts",
    )(packed, w_in, w_out, dec_query[0])

    combined = jnp.dot(combine, back, preferred_element_type=F32)
    enc_rows = inputs + expert_gate[0][:, None] * combined
    enc_out = enc_rows.astype(BF16)
    kv_rows = rms_scale(enc_out.astype(F32), final_gain).astype(BF16)
    context = pl.pallas_call(
        attend_kernel,
        out_shape=jax.ShapeDtypeStruct((q_rows, width), BF16),
        in_specs=[vmem] * 4,
        out_specs=vmem,
        scratch_shapes=[
            pltpu.VMEM((n_seq, tok_rows, 128), BF16),
            pltpu.VMEM((n_seq * tok_rows, 128), BF16),
            pltpu.VMEM((n_seq, q_rows, 128), BF16),
            pltpu.VMEM((n_seq, q_rows, 128), BF16),
        ]
        + [dma((n_seq,))] * 4,
        compiler_params=pltpu.CompilerParams(
            collective_id=1, has_side_effects=True, vmem_limit_bytes=40 << 20
        ),
        name="attend",
    )(kv_rows, w_key, w_value, queries)
    return (enc_out[None], context[None])


def solution(mesh):
    placed = (
        P("exp", "seq", None),
        P("exp", "seq"),
        P("exp", "seq"),
        P("exp", "seq"),
        P(),
        P("exp", None, "seq"),
        P("exp", "seq", None),
        P(),
        P(),
        P(),
        P("exp", "seq", None),
    )
    return jax.shard_map(
        per_device,
        mesh=mesh,
        in_specs=placed,
        out_specs=(P("exp", "seq", None), P("exp", "seq", None)),
        check_vma=False,
    )
```

time: 461 us -> 219 us (0.48)
  waiting for transfers between devices: 311 us -> 0 us
  Pallas kernels: 0 us -> 206 us
  matrix products: 58 us -> 2.86 us
  blocking collectives: 24.5 us -> 0 us
  local copies, waits for them, and re-layouts: 27.6 us -> 6.46 us
  other arithmetic: 17 us -> 2.12 us
  between operations: 13.9 us -> 0.76 us
  starting transfers between devices: 7.46 us -> 0 us
    pallas_call x0 -> x2, Pallas kernels: none -> 206 us  [the longest x1 155 us: per_device(): pl.pallas_call(moe_kernel, out_shape=(jax.ShapeDtypeStruct((tok_rows, wid...]
    all_gather x3 -> x0, waiting for transfers between devices: 180 us -> none  [the longest x1 74.4 us: per_device(): lax.all_gather(arrived, 'seq', axis=0, tiled=True)]
    reduce_scatter x1 -> x0, waiting for transfers between devices: 115 us -> none  [per_device(): lax.psum_scatter(jnp.einsum('ref,efd->red', hidden, w_out, preferred_elem...]
    dot_general x7 -> x2, matrix products: 58 us -> 2.86 us  [the longest x1 2.38 us: per_device(): packed = jnp.dot(dispatch, normed, preferred_element_type=F32).astype(BF16)]
    all_to_all x1 -> x0, blocking collectives: 24.5 us -> none  [per_device(): lax.all_to_all(packed, 'exp', split_axis=0, concat_axis=0, tiled=True)]
    all_gather x2 -> x0, local copies, waits for them, and re-layouts: 23.5 us -> none  [the longest x1 11.7 us: per_device(): fold_values = lax.all_gather(values, 'seq', axis=0, tiled=True)]
    all_to_all x1 -> x0, waiting for transfers between devices: 15.9 us -> none  [per_device(): lax.all_to_all(result, 'exp', split_axis=0, concat_axis=0, tiled=True)]
    reduce_sum x1 -> x0, other arithmetic: 13.5 us -> none  [per_device(): new_sum = jnp.sum(expo, axis=-1)]
  transfers between devices with their start and end apart: 5 -> 0, of which waited for: 5 -> 0; matrix products, arithmetic and copies ran while one was open for 10% -> 0% of each run, Pallas kernels for 0% -> 0%
where the time goes in v1:
time: 219 us; the launch traced here: 218 us
  Pallas kernels  206 us (94%)
  local copies, waits for them, and re-layouts  6.46 us (3%)
  matrix products  2.86 us (1%)
    pallas_call x1, Pallas kernels, per_device(): pl.pallas_call(moe_kernel, out_shape=(jax.ShapeDtypeStruct((tok_rows, wid...  155 us
    pallas_call x1, Pallas kernels, per_device(): pl.pallas_call(attend_kernel, out_shape=jax.ShapeDtypeStruct((q_rows, wid...  51.3 us
    unnamed x20, local copies, waits for them, and re-layouts  6.46 us

profile of v1, /device:TPU:2, one launch (start us, length us, event | category | flops | bytes accessed | tf_op | source)
XLA Modules:
  0.0 218.4 jit_solution(8110226987390011339)
XLA Ops:
  0.6 0.7 compare_select_fusion
  1.3 1.2 fusion.4
  2.6 0.0 copy-start.2
  2.6 2.4 %convolution_convert_fusion.packed_ref = bf16[256,1024]{1,0:T(8,128)(2,1)} fusion(bf16[1,256,1024]{2,1,0:T(8,128)(2,1)} %param.11, f32[1024]{0:T(1024)} %param.15, f32[256]{0:T(256)S(1)} %add_rsqrt_fusion.1, s32[256]{0:T(256)S(1)} %bitcast.17), kind=kOutput, calls=%fused_computation.6 | convolution fusion | flops 135593984 | bytes 1054720 | tf_op jit(solution)/shard_map/dot_general | solution.py:351
  5.0 2.7 %copy.13.win_ref = bf16[4,1024,176]{2,1,0:T(8,128)(2,1)S(1)} copy(bf16[4,1024,176]{1,2,0:T(8,128)(2,1)} %param.16) | data formatting | bytes 2883584 | tf_op args[5]
  7.7 0.0 copy-done.2
  7.7 0.0 copy-start.3
  7.7 1.0 copy-done.3
  8.7 0.0 copy-start.4
  8.7 0.9 copy-done.4
  9.7 0.0 copy-start.6
  9.7 0.0 copy-start.8
  9.7 0.0 copy-start.7
  9.7 0.0 copy-start.1
  9.7 154.8 %experts.1 = (bf16[256,1024]{1,0:T(8,128)(2,1)S(1)}, bf16[16,128,128]{2,1,0:T(8,128)(2,1)S(1)}) custom-call(bf16[256,1024]{1,0:T(8,128)(2,1)S(1)} %copy-done.3, bf16[4,1024,176]{2,1,0:T(8,128)(2,1)S(1)} %copy.13.win_ref, bf16[4,176,1024]{2,1,0:T(8,128)(2,1)S(1)} %copy-done.2, bf16[128,1024]{1,0:T(8,128)(2,1)S(1)} %bitcast.15), custom_call_target="tpu_custom_call" | custom-call | tf_op jit(solution)/shard_map/experts/pallas_call | solution.py:356
  164.5 0.0 copy-start
  164.5 0.0 copy-done.6
  164.5 0.0 copy-done.8
  164.6 0.5 fusion.1
  165.0 0.0 copy-start.5
  165.1 0.0 copy-done.7
  165.1 0.2 fusion.3.rows_ref
  165.3 0.0 copy-done.1
  165.3 1.0 copy-done
  166.3 51.3 %attend.1 = bf16[128,1024]{1,0:T(8,128)(2,1)S(1)} custom-call(bf16[256,1024]{1,0:T(8,128)(2,1)S(1)} %fusion.3.rows_ref, bf16[1024,1024]{1,0:T(8,128)(2,1)S(1)} %copy-done, bf16[1024,1024]{1,0:T(8,128)(2,1)S(1)} %copy-done.1, bf16[16,128,128]{2,1,0:T(8,128)(2,1)S(1)} %get-tuple-element.5.q_ref), custom_call_target="tpu_custom_call" | custom-call | tf_op jit(solution)/shard_map/attend/pallas_call | solution.py:397
  217.6 0.0 copy-done.5
  217.7 0.7 copy.15
  (2 shorter events, 0.0 us)
Async XLA Ops:
  2.6 5.1 %copy-start.2 = (bf16[4,176,1024]{2,1,0:T(8,128)(2,1)S(1)}, bf16[4,176,1024]{2,1,0:T(8,128)(2,1)}, u32[]{:S(2)}) copy-start(bf16[4,176,1024]{2,1,0:T(8,128)(2,1)} %wout_ref.1) | copy-start | bytes 4325380
  7.7 1.0 copy-start.3
  8.7 0.9 copy-start.4
  9.7 154.9 %copy-start.6 = (bf16[1,256,1024]{2,1,0:T(8,128)(2,1)S(1)}, bf16[1,256,1024]{2,1,0:T(8,128)(2,1)}, u32[]{:S(2)}) copy-start(bf16[1,256,1024]{2,1,0:T(8,128)(2,1)} %param.11) | copy-start | bytes 1572868
  9.7 154.9 %copy-start.8 = (f32[1,256]{1,0:T(1,128)S(1)}, f32[1,256]{1,0:T(1,128)}, u32[]{:S(2)}) copy-start(f32[1,256]{1,0:T(1,128)} %param.14) | copy-start | bytes 3076
  9.7 155.4 %copy-start.7 = (f32[1024]{0:T(1024)S(1)}, f32[1024]{0:T(1024)}, u32[]{:S(2)}) copy-start(f32[1024]{0:T(1024)} %param.18) | copy-start | bytes 12292
  9.7 155.6 %copy-start.1 = (bf16[1024,1024]{1,0:T(8,128)(2,1)S(1)}, bf16[1024,1024]{1,0:T(8,128)(2,1)}, u32[]{:S(2)}) copy-start(bf16[1024,1024]{1,0:T(8,128)(2,1)} %wv_ref.1) | copy-start | bytes 6291460
  164.5 1.8 copy-start
  165.0 52.6 %copy-start.5 = (bf16[256,1024]{1,0:T(8,128)(2,1)}, bf16[256,1024]{1,0:T(8,128)(2,1)S(1)}, u32[]{:S(2)}) copy-start(bf16[256,1024]{1,0:T(8,128)(2,1)S(1)} %get-tuple-element.7) | copy-start | bytes 1572868

commit v2 on v1

--- a/solution.py
+++ b/solution.py
@@ -22,7 +22,7 @@
     return pl.ds(pl.multiple_of(index * count, count), count)
 
 
-def greet(axes):
+def signal_all(axes):
     barrier = pltpu.get_barrier_semaphore()
     total = 0
     for axis in axes:
@@ -37,7 +37,7 @@
             return carry
 
         lax.fori_loop(1, n, signal, 0)
-    pl.semaphore_wait(barrier, total)
+    return barrier, total
 
 
 class Exchange:
@@ -80,96 +80,142 @@
         self.loop(lambda d: self.copy(d, self.me).wait_send())
 
 
+def remote(src, dst, send, recv, seq):
+    return pltpu.make_async_remote_copy(
+        src_ref=src,
+        dst_ref=dst,
+        send_sem=send,
+        recv_sem=recv,
+        device_id={"seq": seq},
+        device_id_type=MESH,
+    )
+
+
 def moe_kernel(
-    packed_ref,
+    enc_ref,
+    ids_ref,
+    slots_ref,
+    gain_ref,
     win_ref,
     wout_ref,
     q_ref,
     back_ref,
     qland_ref,
+    enc,
+    query,
+    packed,
     zland,
     rows,
     rland,
     win_land,
     wout_land,
     part,
-    pland,
+    half_up,
+    half_down,
+    full_up,
+    full_down,
     brows,
+    gback,
     zback,
     bland,
     qsend,
     local_sem,
     z_send,
     z_recv,
+    b_send,
+    b_recv,
+    q_send,
+    q_recv,
     wi_send,
     wi_recv,
     wo_send,
     wo_recv,
-    r_send,
-    r_recv,
-    p_send,
-    p_recv,
-    b_send,
-    b_recv,
-    q_send,
-    q_recv,
+    g_send,
+    g_recv,
+    up_send,
+    up_recv,
+    down_send,
+    down_recv,
+    fwd_send,
+    fwd_recv,
+    h_send,
+    h_recv,
+    f_send,
+    f_recv,
+    gb_send,
+    gb_recv,
 ):
     seq, exp = lax.axis_index("seq"), lax.axis_index("exp")
-    n_seq = lax.axis_size("seq")
+    n_seq, n_exp = lax.axis_size("seq"), lax.axis_size("exp")
     experts = win_ref.shape[0]
-    share = n_seq // experts
-    my_y, my_x = seq // share, lax.rem(seq, share)
-    zrows = packed_ref.shape[0] // lax.axis_size("exp")
-    srows = packed_ref.shape[0] // experts
-    greet(("seq", "exp"))
+    hidden_part = win_ref.shape[1]
+    tok = enc_ref.shape[0]
+    zrows, srows = tok // n_exp, tok // experts
+    capacity = zrows // experts
+    core = lax.rem(exp, 2)
+    y, x = seq // experts, lax.rem(seq, experts)
+    line, rank = y + core * (x - y), x + core * (y - x)
+
+    def at(g, r):
+        return g * (experts - core * (experts - 1)) + r * (1 + core * (experts - 1))
+
+    def turn(value, d):
+        return lax.rem(value + experts + d, experts)
+
+    enc_in = pltpu.make_async_copy(enc_ref, enc, local_sem.at[0])
+    q_in = pltpu.make_async_copy(q_ref, query, local_sem.at[1])
+    enc_in.start()
+    q_in.start()
+    barrier, greeted = signal_all(("seq", "exp"))
+    own_weights = [
+        pltpu.make_async_copy(
+            ref.at[line], land.at[rows_at(line, hidden_part)], local_sem.at[2 + i]
+        )
+        for i, (ref, land) in enumerate(((win_ref, win_land), (wout_ref, wout_land)))
+    ]
+    for copy in own_weights:
+        copy.start()
+    enc_in.wait()
+    normed = rms_scale(enc[...].astype(F32), gain_ref[...]).astype(BF16)
+    target = jnp.where(slots_ref[...] < capacity, ids_ref[...] * capacity + slots_ref[...], -1)
+    out_row = lax.broadcasted_iota(jnp.int32, (tok, tok), 0)
+    in_row = lax.broadcasted_iota(jnp.int32, (tok, tok), 1)
+    dispatch = (out_row == target).astype(BF16)
+    packed[...] = jnp.dot(dispatch, normed, preferred_element_type=F32).astype(BF16)
+    pl.semaphore_wait(barrier, greeted)
 
     z_out = Exchange(
         "exp",
-        lambda t: packed_ref.at[rows_at(t, zrows)],
+        lambda t: packed.at[rows_at(t, zrows)],
         lambda s: zland.at[rows_at(s, zrows)],
         z_send,
         z_recv,
     )
     z_out.start()
-    zland[rows_at(exp, zrows), :] = packed_ref[rows_at(exp, zrows), :]
 
     def weight_copy(d, slot, ref, land, send, recv):
-        k = lax.rem(my_y + d, experts)
-        return pltpu.make_async_remote_copy(
-            src_ref=ref.at[k],
-            dst_ref=land.at[slot],
-            send_sem=send.at[d],
-            recv_sem=recv.at[d],
-            device_id={"seq": k * share + my_x},
-            device_id_type=MESH,
+        k = turn(line, d)
+        return remote(
+            ref.at[k], land.at[rows_at(slot, hidden_part)], send.at[d], recv.at[d], at(k, rank)
         )
 
     weights = ((win_ref, win_land, wi_send, wi_recv), (wout_ref, wout_land, wo_send, wo_recv))
-    for d in range(1, experts):
-        for each in weights:
-            weight_copy(d, my_y, *each).start()
-    own = [
-        pltpu.make_async_copy(ref.at[my_y], land.at[my_y], local_sem.at[i])
-        for i, (ref, land, _, _) in enumerate(weights)
-    ]
-    for copy in own:
-        copy.start()
-
+    for each in weights:
+        for d in range(1, experts):
+            weight_copy(d, line, *each).start()
+    zland[rows_at(exp, zrows), :] = packed[rows_at(exp, zrows), :]
+
+    q_in.wait()
     lane = lax.broadcasted_iota(jnp.int32, (q_ref.shape[0], 128), 1)
     for p in range(HEADS // 2):
-        pair = pltpu.roll(q_ref[:, p * 128 : (p + 1) * 128].astype(F32) * 0.125, 64, 1)
+        pair = pltpu.roll(query[:, p * 128 : (p + 1) * 128].astype(F32) * 0.125, 64, 1)
         qsend[2 * p] = jnp.where(lane >= 64, pair, 0.0).astype(BF16)
         qsend[2 * p + 1] = jnp.where(lane < 64, pair, 0.0).astype(BF16)
     q_out = Exchange(
         "seq", lambda t: qsend.at[t], lambda s: qland_ref.at[s], q_send, q_recv
     )
-    q_own = pltpu.make_async_copy(qsend.at[seq], qland_ref.at[seq], local_sem.at[2])
+    q_own = pltpu.make_async_copy(qsend.at[seq], qland_ref.at[seq], local_sem.at[0])
     q_own.start()
-
-    total = packed_ref.shape[0]
-    capacity = zrows // experts
-    out_row = lax.broadcasted_iota(jnp.int32, (total, total), 0)
-    in_row = lax.broadcasted_iota(jnp.int32, (total, total), 1)
 
     def by_expert(r):
         j, k, c = r // zrows, lax.rem(r // capacity, experts), lax.rem(r, capacity)
@@ -177,59 +223,135 @@
 
     forward = (by_expert(in_row) == out_row).astype(BF16)
     inverse = (by_expert(out_row) == in_row).astype(BF16)
-
     z_out.arrived()
     rows[...] = jnp.dot(forward, zland[...], preferred_element_type=F32).astype(BF16)
 
-    r_out = Exchange(
-        "seq",
-        lambda t: rows.at[rows_at(t // share, srows)],
-        lambda s: rland.at[rows_at(s, srows)],
-        r_send,
-        r_recv,
-    )
-    r_out.start()
-    q_out.start()
-    rland[rows_at(seq, srows), :] = rows[rows_at(my_y, srows), :]
-    for copy in own:
+    def piece(r, g):
+        return rland.at[r, rows_at(g, srows)]
+
+    def to_line(d, slot):
+        k = turn(line, d)
+        return remote(
+            rows.at[rows_at(k, srows)], piece(rank, slot), g_send.at[d], g_recv.at[d], at(k, rank)
+        )
+
+    def up(d, r):
+        g = turn(line, -d)
+        return remote(
+            piece(rank, g), piece(r, g), up_send.at[d], up_recv.at[d], at(line, turn(rank, 1))
+        )
+
+    def down(d, r):
+        g = turn(line, -d)
+        return remote(
+            piece(rank, g), piece(r, g), down_send.at[d], down_recv.at[d], at(line, turn(rank, -1))
+        )
+
+    def forwarded(d, r):
+        g = turn(line, -d)
+        way = 1 if d < 2 else -1
+        return remote(
+            piece(turn(rank, -way), g),
+            piece(r, g),
+            fwd_send.at[d],
+            fwd_recv.at[d],
+            at(line, turn(rank, way)),
+        )
+
+    for d in range(1, experts):
+        to_line(d, line).start()
+    rland[rank, rows_at(line, srows), :] = rows[rows_at(line, srows), :]
+    for d in range(experts):
+        if d:
+            to_line(d, turn(line, -d)).wait_recv()
+        up(d, rank).start()
+        down(d, rank).start()
+    for copy in own_weights:
         copy.wait()
     for d in range(1, experts):
-        slot = lax.rem(my_y + experts - d, experts)
         for each in weights:
-            weight_copy(d, slot, *each).wait_recv()
-    r_out.arrived()
-
-    tile = 256
-
-    def ffn(m, carry):
-        block = rland[rows_at(m, tile), :]
-        acc = None
-        for h in range(experts):
-            product = jnp.dot(block, win_land[h], preferred_element_type=F32)
-            hidden = jnp.maximum(product, 0.0).astype(BF16)
-            term = jnp.dot(hidden, wout_land[h], preferred_element_type=F32)
-            acc = term if acc is None else acc + term
-        part[rows_at(m, tile), :] = acc
-        return carry
-
-    lax.fori_loop(0, rland.shape[0] // tile, ffn, 0)
-
-    p_out = Exchange(
-        "seq",
-        lambda t: part.at[rows_at(t, srows)],
-        lambda s: pland.at[s],
-        p_send,
-        p_recv,
-    )
-    p_out.start()
-    pland[seq] = part[rows_at(seq, srows), :]
-    p_out.arrived()
-    for k in range(experts):
-        acc = pland[k * share]
-        for i in range(1, share):
-            acc = acc + pland[k * share + i]
-        brows[k * srows : (k + 1) * srows, :] = acc.astype(BF16)
-    zback[...] = jnp.dot(inverse, brows[...], preferred_element_type=F32).astype(BF16)
+            weight_copy(d, turn(line, -d), *each).wait_recv()
+
+    def ffn(r):
+        product = lax.dot_general(
+            rland[r], win_land[...], (((1,), (1,)), ((), ())), preferred_element_type=F32
+        )
+        hidden = jnp.maximum(product, 0.0).astype(BF16)
+        part[r] = jnp.dot(hidden, wout_land[...], preferred_element_type=F32)
+
+    above, below, across = turn(rank, 1), turn(rank, -1), turn(rank, 2)
+    for d in (0, 1):
+        up(d, below).wait_recv()
+        forwarded(d, below).start()
+    ffn(rank)
+    for d in (2, 3):
+        down(d, above).wait_recv()
+        forwarded(d, above).start()
+    for d in (2, 3):
+        up(d, below).wait_recv()
+    ffn(below)
+    for d in (0, 1):
+        down(d, above).wait_recv()
+    ffn(above)
+    for d in range(experts):
+        forwarded(d, across).wait_recv()
+    ffn(across)
+
+    mid = tok // 2
+    first, second = pl.ds(0, mid), pl.ds(mid, mid)
+    far_up = remote(
+        part.at[across, first], half_up, h_send.at[0], h_recv.at[0], at(line, above)
+    )
+    far_down = remote(
+        part.at[across, second], half_down, h_send.at[1], h_recv.at[1], at(line, below)
+    )
+    near = [
+        remote(part.at[r, rows_], land.at[rows_], f_send.at[i], f_recv.at[i], at(line, r))
+        for i, (r, rows_, land) in enumerate(
+            (
+                (above, second, full_up),
+                (below, first, full_down),
+                (above, first, full_up),
+                (below, second, full_down),
+            )
+        )
+    ]
+    far_up.start()
+    far_down.start()
+    near[0].start()
+    near[1].start()
+    far_up.wait_recv()
+    part[above, first, :] = part[above, first, :] + half_up[...]
+    near[2].start()
+    far_down.wait_recv()
+    part[below, second, :] = part[below, second, :] + half_down[...]
+    near[3].start()
+    near[0].wait_recv()
+    near[3].wait_recv()
+    brows[second, :] = (part[rank, second, :] + full_up[second, :] + full_down[second, :]).astype(
+        BF16
+    )
+    near[1].wait_recv()
+    near[2].wait_recv()
+    brows[first, :] = (part[rank, first, :] + full_up[first, :] + full_down[first, :]).astype(BF16)
+
+    def from_line(d, slot):
+        g = turn(line, d)
+        return remote(
+            brows.at[rows_at(g, srows)],
+            gback.at[rows_at(slot, srows)],
+            gb_send.at[d],
+            gb_recv.at[d],
+            at(g, rank),
+        )
+
+    for d in range(1, experts):
+        from_line(d, line).start()
+    gback[rows_at(line, srows), :] = brows[rows_at(line, srows), :]
+    q_out.start()
+    for d in range(1, experts):
+        from_line(d, turn(line, -d)).wait_recv()
+    zback[...] = jnp.dot(inverse, gback[...], preferred_element_type=F32).astype(BF16)
 
     b_out = Exchange(
         "exp",
@@ -244,11 +366,19 @@
     q_out.arrived()
     b_out.arrived()
     back_ref[...] = bland[...]
-    for exchange in (z_out, r_out, q_out, p_out, b_out):
+    for exchange in (z_out, q_out, b_out):
         exchange.sent()
     for d in range(1, experts):
         for each in weights:
-            weight_copy(d, my_y, *each).wait_send()
+            weight_copy(d, line, *each).wait_send()
+        to_line(d, line).wait_send()
+        from_line(d, line).wait_send()
+    for d in range(experts):
+        up(d, rank).wait_send()
+        down(d, rank).wait_send()
+        forwarded(d, rank).wait_send()
+    for copy in (far_up, far_down, *near):
+        copy.wait_send()
 
 
 def attend_kernel(
@@ -269,7 +399,8 @@
     seq = lax.axis_index("seq")
     n_seq = lax.axis_size("seq")
     count = rows_ref.shape[0]
-    greet(("seq",))
+    barrier, greeted = signal_all(("seq",))
+    pl.semaphore_wait(barrier, greeted)
     lane = lax.broadcasted_iota(jnp.int32, (count, 128), 1)
     low = lane < 64
     block = rows_ref[...]
@@ -339,57 +470,68 @@
     tok_rows, width = enc_in.shape[1:]
     experts, _, part_ff = w_in.shape
     capacity = tok_rows // (experts * n_exp)
-    srows = tok_rows // experts
     q_rows = dec_query.shape[1]
-    inputs = enc_in[0].astype(F32)
-    normed = rms_scale(inputs, moe_gain).astype(BF16)
-    kept = slots[0] < capacity
-    target = jnp.where(kept, expert_ids[0] * capacity + slots[0], -1)
-    places = jnp.arange(tok_rows, dtype=jnp.int32)
-    dispatch = (places[:, None] == target[None, :]).astype(BF16)
-    combine = (target[:, None] == places[None, :]).astype(BF16)
-    packed = jnp.dot(dispatch, normed, preferred_element_type=F32).astype(BF16)
 
     vmem = pl.BlockSpec(memory_space=pltpu.VMEM)
     hbm = pl.BlockSpec(memory_space=pl.ANY)
     dma = pltpu.SemaphoreType.DMA
+    whole = pltpu.VMEM((tok_rows, width), BF16)
+    half = pltpu.VMEM((tok_rows // 2, width), F32)
+    full = pltpu.VMEM((tok_rows, width), F32)
+    weight = pltpu.VMEM((experts * part_ff, width), BF16)
     back, queries = pl.pallas_call(
         moe_kernel,
         out_shape=(
             jax.ShapeDtypeStruct((tok_rows, width), BF16),
             jax.ShapeDtypeStruct((n_seq, q_rows, 128), BF16),
         ),
-        in_specs=[vmem, hbm, hbm, vmem],
+        in_specs=[hbm, vmem, vmem, vmem, hbm, hbm, hbm],
         out_specs=(vmem, hbm),
         scratch_shapes=[
-            pltpu.VMEM((tok_rows, width), BF16),
-            pltpu.VMEM((tok_rows, width), BF16),
-            pltpu.VMEM((n_seq * srows, width), BF16),
-            pltpu.VMEM((experts, width, part_ff), BF16),
-            pltpu.VMEM((experts, part_ff, width), BF16),
-            pltpu.VMEM((n_seq * srows, width), F32),
-            pltpu.VMEM((n_seq, srows, width), F32),
-            pltpu.VMEM((tok_rows, width), BF16),
-            pltpu.VMEM((tok_rows, width), BF16),
-            pltpu.VMEM((tok_rows, width), BF16),
+            whole,
+            pltpu.VMEM((q_rows, width), BF16),
+            whole,
+            whole,
+            whole,
+            pltpu.VMEM((experts, tok_rows, width), BF16),
+            weight,
+            weight,
+            pltpu.VMEM((experts, tok_rows, width), F32),
+            half,
+            half,
+            full,
+            full,
+            whole,
+            whole,
+            whole,
+            whole,
             pltpu.VMEM((n_seq, q_rows, 128), BF16),
-            dma((3,)),
-            dma((n_exp,)),
-            dma((n_exp,)),
-            dma((experts,)),
-            dma((experts,)),
-            dma((experts,)),
-            dma((experts,)),
+            dma((4,)),
         ]
-        + [dma((n_seq,))] * 4
-        + [dma((n_exp,))] * 2
-        + [dma((n_seq,))] * 2,
+        + [dma((n_exp,))] * 4
+        + [dma((n_seq,))] * 2
+        + [dma((experts,))] * 12
+        + [dma((2,))] * 2
+        + [dma((4,))] * 2
+        + [dma((experts,))] * 2,
         compiler_params=pltpu.CompilerParams(
-            collective_id=0, has_side_effects=True, vmem_limit_bytes=40 << 20
+            collective_id=0, has_side_effects=True, vmem_limit_bytes=56 << 20
         ),
         name="experts",
-    )(packed, w_in, w_out, dec_query[0])
-
+    )(
+        enc_in[0],
+        expert_ids,
+        slots,
+        moe_gain[None],
+        jnp.swapaxes(w_in, 1, 2),
+        w_out,
+        dec_query[0],
+    )
+
+    inputs = enc_in[0].astype(F32)
+    places = jnp.arange(tok_rows, dtype=jnp.int32)
+    target = jnp.where(slots[0] < capacity, expert_ids[0] * capacity + slots[0], -1)
+    combine = (target[:, None] == places[None, :]).astype(BF16)
     combined = jnp.dot(combine, back, preferred_element_type=F32)
     enc_rows = inputs + expert_gate[0][:, None] * combined
     enc_out = enc_rows.astype(BF16)

time: 219 us -> 132 us (0.60)
  Pallas kernels: 206 us -> 127 us
  local copies, waits for them, and re-layouts: 6.46 us -> 0.74 us
    pallas_call x1, Pallas kernels: 155 us -> 88.1 us  [per_device(): pl.pallas_call(moe_kernel, out_shape=(jax.ShapeDtypeStruct((tok_rows, wid...]
    pallas_call x1, Pallas kernels: 51.3 us -> 39 us  [per_device(): pl.pallas_call(attend_kernel, out_shape=jax.ShapeDtypeStruct((q_rows, wid...]
    unnamed x20 -> x15, local copies, waits for them, and re-layouts: 6.46 us -> 0.74 us
    dot_general x1 -> x0, matrix products: 2.38 us -> none  [per_device(): packed = jnp.dot(dispatch, normed, preferred_element_type=F32).astype(BF16)]
where the time goes in v2:
time: 132 us; the launch traced here: 131 us
  Pallas kernels  127 us (96%)
  matrix products  1.67 us (1%)
    pallas_call x1, Pallas kernels, per_device(): pl.pallas_call(moe_kernel, out_shape=(jax.ShapeDtypeStruct((tok_rows, wid...  88.1 us
    pallas_call x1, Pallas kernels, per_device(): pl.pallas_call(attend_kernel, out_shape=jax.ShapeDtypeStruct((q_rows, wid...  39 us

profile of v2, /device:TPU:2, one launch (start us, length us, event | category | flops | bytes accessed | tf_op | source)
XLA Modules:
  0.0 131.2 jit_solution(12408891126124647040)
XLA Ops:
  0.6 0.0 copy-start.4
  0.6 0.0 copy-start.6
  0.7 0.8 compare_select_fusion
  1.4 0.0 copy-start.5
  1.4 0.0 copy-start.1
  1.4 88.1 %experts.1 = (bf16[256,1024]{1,0:T(8,128)(2,1)}, bf16[16,128,128]{2,1,0:T(8,128)(2,1)}) custom-call(bf16[256,1024]{1,0:T(8,128)(2,1)} %bitcast.13, s32[1,256]{1,0:T(1,128)} %ids_ref.1, s32[1,256]{1,0:T(1,128)} %slots_ref.1, f32[1,1024]{1,0:T(1,128)} %bitcast.15, bf16[4,176,1024]{2,1,0:T(8,128)(2,1)} %bitcast.11, bf16[4,176,1024]{2,1,0:T(8,128)(2,1)} %wout_ref.1, ...), custom_call_target="tpu_custom_call" | custom-call | tf_op jit(solution)/shard_map/experts/pallas_call | solution.py:482
  89.6 0.0 copy-start
  89.6 0.0 copy-start.2
  89.6 0.0 copy-done.4
  89.6 0.0 copy-done.6
  89.6 1.7 %fusion.2 = (f32[256]{0:T(256)S(1)}, bf16[256,1024]{1,0:T(8,128)(2,1)S(1)}) fusion(bf16[256,1024]{1,0:T(8,128)(2,1)} %get-tuple-element.4, s32[256]{0:T(256)S(1)} %bitcast.16, f32[256]{0:T(256)S(1)} %bitcast.17, bf16[1,256,1024]{2,1,0:T(8,128)(2,1)S(1)} %copy-done.4), kind=kOutput, calls=%fused_computation.5 | convolution fusion | flops 136118016 | bytes 1575936 | tf_op jit(solution)/shard_map/dot_general | solution.py:535
  91.3 0.0 copy-start.3
  91.3 0.0 copy-done.5
  91.3 0.2 fusion.4.rows_ref
  91.5 0.0 copy-done.1
  91.5 0.0 copy-done
  91.5 0.0 copy-done.2
  91.5 39.0 %attend.1 = bf16[128,1024]{1,0:T(8,128)(2,1)S(1)} custom-call(bf16[256,1024]{1,0:T(8,128)(2,1)S(1)} %fusion.4.rows_ref, bf16[1024,1024]{1,0:T(8,128)(2,1)S(1)} %copy-done, bf16[1024,1024]{1,0:T(8,128)(2,1)S(1)} %copy-done.1, bf16[16,128,128]{2,1,0:T(8,128)(2,1)S(1)} %copy-done.2), custom_call_target="tpu_custom_call" | custom-call | tf_op jit(solution)/shard_map/attend/pallas_call | solution.py:539
  130.5 0.0 copy-done.3
  130.5 0.7 copy.14
  (1 shorter events, 0.0 us)
Async XLA Ops:
  0.6 89.0 %copy-start.4 = (bf16[1,256,1024]{2,1,0:T(8,128)(2,1)S(1)}, bf16[1,256,1024]{2,1,0:T(8,128)(2,1)}, u32[]{:S(2)}) copy-start(bf16[1,256,1024]{2,1,0:T(8,128)(2,1)} %param.11) | copy-start | bytes 1572868
  0.6 89.0 %copy-start.6 = (f32[1,256]{1,0:T(1,128)S(1)}, f32[1,256]{1,0:T(1,128)}, u32[]{:S(2)}) copy-start(f32[1,256]{1,0:T(1,128)} %param.14) | copy-start | bytes 3076
  1.4 89.9 %copy-start.5 = (f32[1024]{0:T(1024)S(1)}, f32[1024]{0:T(1024)}, u32[]{:S(2)}) copy-start(f32[1024]{0:T(1024)} %param.18) | copy-start | bytes 12292
  1.4 90.1 %copy-start.1 = (bf16[1024,1024]{1,0:T(8,128)(2,1)S(1)}, bf16[1024,1024]{1,0:T(8,128)(2,1)}, u32[]{:S(2)}) copy-start(bf16[1024,1024]{1,0:T(8,128)(2,1)} %wv_ref.1) | copy-start | bytes 6291460
  89.6 2.0 %copy-start = (bf16[1024,1024]{1,0:T(8,128)(2,1)S(1)}, bf16[1024,1024]{1,0:T(8,128)(2,1)}, u32[]{:S(2)}) copy-start(bf16[1024,1024]{1,0:T(8,128)(2,1)} %wk_ref.1) | copy-start | bytes 6291460
  89.6 2.0 %copy-start.2 = (bf16[16,128,128]{2,1,0:T(8,128)(2,1)S(1)}, bf16[16,128,128]{2,1,0:T(8,128)(2,1)}, u32[]{:S(2)}) copy-start(bf16[16,128,128]{2,1,0:T(8,128)(2,1)} %get-tuple-element.5.q_ref) | copy-start | bytes 1572868
  91.3 39.2 %copy-start.3 = (bf16[256,1024]{1,0:T(8,128)(2,1)}, bf16[256,1024]{1,0:T(8,128)(2,1)S(1)}, u32[]{:S(2)}) copy-start(bf16[256,1024]{1,0:T(8,128)(2,1)S(1)} %get-tuple-element.7) | copy-start | bytes 1572868

commit v3 on v2

--- a/solution.py
+++ b/solution.py
@@ -8,6 +8,7 @@
 from jax.sharding import PartitionSpec as P
 
 HEADS = 16
+CHUNKS = 2
 MESH = pl.DeviceIdType.MESH
 F32 = jnp.float32
 BF16 = jnp.bfloat16
@@ -109,6 +110,8 @@
     rland,
     win_land,
     wout_land,
+    relay,
+    hidden,
     part,
     half_up,
     half_down,
@@ -130,6 +133,8 @@
     wi_recv,
     wo_send,
     wo_recv,
+    relay_send,
+    relay_recv,
     g_send,
     g_recv,
     up_send,
@@ -184,14 +189,20 @@
     packed[...] = jnp.dot(dispatch, normed, preferred_element_type=F32).astype(BF16)
     pl.semaphore_wait(barrier, greeted)
 
-    z_out = Exchange(
-        "exp",
-        lambda t: packed.at[rows_at(t, zrows)],
-        lambda s: zland.at[rows_at(s, zrows)],
-        z_send,
-        z_recv,
-    )
-    z_out.start()
+    chunks = z_send.shape[0]
+    wide = enc_ref.shape[1] // chunks
+
+    def cols(c):
+        return pl.ds(c * wide, wide)
+
+    def z_out(c):
+        return Exchange(
+            "exp",
+            lambda t: packed.at[rows_at(t, zrows), cols(c)],
+            lambda s: zland.at[rows_at(s, zrows), cols(c)],
+            z_send.at[c],
+            z_recv.at[c],
+        )
 
     def weight_copy(d, slot, ref, land, send, recv):
         k = turn(line, d)
@@ -199,10 +210,32 @@
             ref.at[k], land.at[rows_at(slot, hidden_part)], send.at[d], recv.at[d], at(k, rank)
         )
 
-    weights = ((win_ref, win_land, wi_send, wi_recv), (wout_ref, wout_land, wo_send, wo_recv))
-    for each in weights:
-        for d in range(1, experts):
-            weight_copy(d, line, *each).start()
+    relay_in = remote(
+        wout_ref.at[turn(line, 2)],
+        relay,
+        relay_send.at[0],
+        relay_recv.at[0],
+        at(turn(line, -1), rank),
+    )
+
+    def relay_out(slot):
+        return remote(
+            relay,
+            wout_land.at[rows_at(slot, hidden_part)],
+            relay_send.at[1],
+            relay_recv.at[1],
+            at(turn(line, -1), rank),
+        )
+
+    w_first = (win_ref, win_land, wi_send, wi_recv)
+    w_second = (wout_ref, wout_land, wo_send, wo_recv)
+    direct = [(d, w_first) for d in range(1, experts)] + [(d, w_second) for d in (1, 3)]
+    z_out(0).start()
+    relay_in.start()
+    for d, each in direct:
+        weight_copy(d, line, *each).start()
+    for c in range(1, chunks):
+        z_out(c).start()
     zland[rows_at(exp, zrows), :] = packed[rows_at(exp, zrows), :]
 
     q_in.wait()
@@ -223,162 +256,224 @@
 
     forward = (by_expert(in_row) == out_row).astype(BF16)
     inverse = (by_expert(out_row) == in_row).astype(BF16)
-    z_out.arrived()
-    rows[...] = jnp.dot(forward, zland[...], preferred_element_type=F32).astype(BF16)
-
-    def piece(r, g):
-        return rland.at[r, rows_at(g, srows)]
-
-    def to_line(d, slot):
+    relay_in.wait_recv()
+    relay_out(turn(line, 1)).start()
+
+    above, below, across = turn(rank, 1), turn(rank, -1), turn(rank, 2)
+
+    def piece(r, g, c):
+        return rland.at[r, rows_at(g, srows), cols(c)]
+
+    def to_line(c, d, slot):
         k = turn(line, d)
         return remote(
-            rows.at[rows_at(k, srows)], piece(rank, slot), g_send.at[d], g_recv.at[d], at(k, rank)
-        )
-
-    def up(d, r):
+            rows.at[rows_at(k, srows), cols(c)],
+            piece(rank, slot, c),
+            g_send.at[c, d],
+            g_recv.at[c, d],
+            at(k, rank),
+        )
+
+    def up(c, d, r):
         g = turn(line, -d)
         return remote(
-            piece(rank, g), piece(r, g), up_send.at[d], up_recv.at[d], at(line, turn(rank, 1))
-        )
-
-    def down(d, r):
+            piece(rank, g, c), piece(r, g, c), up_send.at[c, d], up_recv.at[c, d], at(line, above)
+        )
+
+    def down(c, d, r):
         g = turn(line, -d)
         return remote(
-            piece(rank, g), piece(r, g), down_send.at[d], down_recv.at[d], at(line, turn(rank, -1))
-        )
-
-    def forwarded(d, r):
+            piece(rank, g, c),
+            piece(r, g, c),
+            down_send.at[c, d],
+            down_recv.at[c, d],
+            at(line, below),
+        )
+
+    def forwarded(c, d, r):
         g = turn(line, -d)
         way = 1 if d < 2 else -1
         return remote(
-            piece(turn(rank, -way), g),
-            piece(r, g),
-            fwd_send.at[d],
-            fwd_recv.at[d],
+            piece(turn(rank, -way), g, c),
+            piece(r, g, c),
+            fwd_send.at[c, d],
+            fwd_recv.at[c, d],
             at(line, turn(rank, way)),
         )
 
-    for d in range(1, experts):
-        to_line(d, line).start()
-    rland[rank, rows_at(line, srows), :] = rows[rows_at(line, srows), :]
-    for d in range(experts):
-        if d:
-            to_line(d, turn(line, -d)).wait_recv()
-        up(d, rank).start()
-        down(d, rank).start()
+    for c in range(chunks):
+        z_out(c).arrived()
+        rows[:, cols(c)] = jnp.dot(
+            forward, zland[:, cols(c)], preferred_element_type=F32
+        ).astype(BF16)
+        for d in range(1, experts):
+            to_line(c, d, line).start()
+        rland[rank, rows_at(line, srows), cols(c)] = rows[rows_at(line, srows), cols(c)]
+        for d in range(experts):
+            if d:
+                to_line(c, d, turn(line, -d)).wait_recv()
+            up(c, d, rank).start()
+            down(c, d, rank).start()
+        for d in (0, 1):
+            up(c, d, below).wait_recv()
+            forwarded(c, d, below).start()
+        for d in (2, 3):
+            down(c, d, above).wait_recv()
+            forwarded(c, d, above).start()
+
+    def first_layer(r):
+        product = lax.dot_general(
+            rland[r], win_land[...], (((1,), (1,)), ((), ())), preferred_element_type=F32
+        )
+        hidden[r] = jnp.maximum(product, 0.0).astype(BF16)
+
     for copy in own_weights:
         copy.wait()
-    for d in range(1, experts):
-        for each in weights:
+    for d, each in direct:
+        if each is w_first:
             weight_copy(d, turn(line, -d), *each).wait_recv()
-
-    def ffn(r):
-        product = lax.dot_general(
-            rland[r], win_land[...], (((1,), (1,)), ((), ())), preferred_element_type=F32
-        )
-        hidden = jnp.maximum(product, 0.0).astype(BF16)
-        part[r] = jnp.dot(hidden, wout_land[...], preferred_element_type=F32)
-
-    above, below, across = turn(rank, 1), turn(rank, -1), turn(rank, 2)
-    for d in (0, 1):
-        up(d, below).wait_recv()
-        forwarded(d, below).start()
-    ffn(rank)
-    for d in (2, 3):
-        down(d, above).wait_recv()
-        forwarded(d, above).start()
-    for d in (2, 3):
-        up(d, below).wait_recv()
-    ffn(below)
-    for d in (0, 1):
-        down(d, above).wait_recv()
-    ffn(above)
-    for d in range(experts):
-        forwarded(d, across).wait_recv()
-    ffn(across)
+    first_layer(rank)
+    for c in range(chunks):
+        for d in (2, 3):
+            up(c, d, below).wait_recv()
+    first_layer(below)
+    for c in range(chunks):
+        for d in (0, 1):
+            down(c, d, above).wait_recv()
+    first_layer(above)
+    for c in range(chunks):
+        for d in range(experts):
+            forwarded(c, d, across).wait_recv()
+    first_layer(across)
+    for d, each in direct:
+        if each is w_second:
+            weight_copy(d, turn(line, -d), *each).wait_recv()
+    relay_out(turn(line, 2)).wait_recv()
 
     mid = tok // 2
     first, second = pl.ds(0, mid), pl.ds(mid, mid)
-    far_up = remote(
-        part.at[across, first], half_up, h_send.at[0], h_recv.at[0], at(line, above)
-    )
-    far_down = remote(
-        part.at[across, second], half_down, h_send.at[1], h_recv.at[1], at(line, below)
-    )
-    near = [
-        remote(part.at[r, rows_], land.at[rows_], f_send.at[i], f_recv.at[i], at(line, r))
-        for i, (r, rows_, land) in enumerate(
-            (
-                (above, second, full_up),
-                (below, first, full_down),
-                (above, first, full_up),
-                (below, second, full_down),
+
+    def far(c, way):
+        half, land, r = ((first, half_up, above), (second, half_down, below))[way]
+        return remote(
+            part.at[across, half, cols(c)],
+            land.at[:, cols(c)],
+            h_send.at[c, way],
+            h_recv.at[c, way],
+            at(line, r),
+        )
+
+    def near(c, i):
+        r, half, land = (
+            (above, second, full_up),
+            (below, first, full_down),
+            (above, first, full_up),
+            (below, second, full_down),
+        )[i]
+        return remote(
+            part.at[r, half, cols(c)],
+            land.at[half, cols(c)],
+            f_send.at[c, i],
+            f_recv.at[c, i],
+            at(line, r),
+        )
+
+    def from_line(c, d, slot):
+        g = turn(line, d)
+        return remote(
+            brows.at[rows_at(g, srows), cols(c)],
+            gback.at[rows_at(slot, srows), cols(c)],
+            gb_send.at[c, d],
+            gb_recv.at[c, d],
+            at(g, rank),
+        )
+
+    def b_out(c):
+        return Exchange(
+            "exp",
+            lambda t: zback.at[rows_at(t, zrows), cols(c)],
+            lambda s: bland.at[rows_at(s, zrows), cols(c)],
+            b_send.at[c],
+            b_recv.at[c],
+        )
+
+    def second_layer(c):
+        def one(r):
+            part[r, :, cols(c)] = jnp.dot(
+                hidden[r], wout_land[:, cols(c)], preferred_element_type=F32
             )
-        )
-    ]
-    far_up.start()
-    far_down.start()
-    near[0].start()
-    near[1].start()
-    far_up.wait_recv()
-    part[above, first, :] = part[above, first, :] + half_up[...]
-    near[2].start()
-    far_down.wait_recv()
-    part[below, second, :] = part[below, second, :] + half_down[...]
-    near[3].start()
-    near[0].wait_recv()
-    near[3].wait_recv()
-    brows[second, :] = (part[rank, second, :] + full_up[second, :] + full_down[second, :]).astype(
-        BF16
-    )
-    near[1].wait_recv()
-    near[2].wait_recv()
-    brows[first, :] = (part[rank, first, :] + full_up[first, :] + full_down[first, :]).astype(BF16)
-
-    def from_line(d, slot):
-        g = turn(line, d)
-        return remote(
-            brows.at[rows_at(g, srows)],
-            gback.at[rows_at(slot, srows)],
-            gb_send.at[d],
-            gb_recv.at[d],
-            at(g, rank),
-        )
-
-    for d in range(1, experts):
-        from_line(d, line).start()
-    gback[rows_at(line, srows), :] = brows[rows_at(line, srows), :]
+
+        one(across)
+        far(c, 0).start()
+        far(c, 1).start()
+        one(above)
+        near(c, 0).start()
+        one(below)
+        near(c, 1).start()
+        one(rank)
+
+    def add_far(c):
+        far(c, 0).wait_recv()
+        part[above, first, cols(c)] = part[above, first, cols(c)] + half_up[:, cols(c)]
+        near(c, 2).start()
+        far(c, 1).wait_recv()
+        part[below, second, cols(c)] = part[below, second, cols(c)] + half_down[:, cols(c)]
+        near(c, 3).start()
+
+    def finish(c):
+        for i in (0, 1, 2, 3):
+            near(c, i).wait_recv()
+        brows[:, cols(c)] = (
+            part[rank, :, cols(c)] + full_up[:, cols(c)] + full_down[:, cols(c)]
+        ).astype(BF16)
+        for d in range(1, experts):
+            from_line(c, d, line).start()
+        gback[rows_at(line, srows), cols(c)] = brows[rows_at(line, srows), cols(c)]
+
+    def give_back(c):
+        for d in range(1, experts):
+            from_line(c, d, turn(line, -d)).wait_recv()
+        zback[:, cols(c)] = jnp.dot(
+            inverse, gback[:, cols(c)], preferred_element_type=F32
+        ).astype(BF16)
+        b_out(c).start()
+        bland[rows_at(exp, zrows), cols(c)] = zback[rows_at(exp, zrows), cols(c)]
+
+    second_layer(0)
+    add_far(0)
+    for c in range(1, chunks):
+        second_layer(c)
+        finish(c - 1)
+        add_far(c)
+        give_back(c - 1)
+    finish(chunks - 1)
     q_out.start()
-    for d in range(1, experts):
-        from_line(d, turn(line, -d)).wait_recv()
-    zback[...] = jnp.dot(inverse, gback[...], preferred_element_type=F32).astype(BF16)
-
-    b_out = Exchange(
-        "exp",
-        lambda t: zback.at[rows_at(t, zrows)],
-        lambda s: bland.at[rows_at(s, zrows)],
-        b_send,
-        b_recv,
-    )
-    b_out.start()
-    bland[rows_at(exp, zrows), :] = zback[rows_at(exp, zrows), :]
+    give_back(chunks - 1)
+
     q_own.wait()
     q_out.arrived()
-    b_out.arrived()
+    for c in range(chunks):
+        b_out(c).arrived()
     back_ref[...] = bland[...]
-    for exchange in (z_out, q_out, b_out):
-        exchange.sent()
-    for d in range(1, experts):
-        for each in weights:
-            weight_copy(d, line, *each).wait_send()
-        to_line(d, line).wait_send()
-        from_line(d, line).wait_send()
-    for d in range(experts):
-        up(d, rank).wait_send()
-        down(d, rank).wait_send()
-        forwarded(d, rank).wait_send()
-    for copy in (far_up, far_down, *near):
-        copy.wait_send()
+    q_out.sent()
+    for d, each in direct:
+        weight_copy(d, line, *each).wait_send()
+    relay_in.wait_send()
+    relay_out(line).wait_send()
+    for c in range(chunks):
+        z_out(c).sent()
+        b_out(c).sent()
+        for d in range(experts):
+            if d:
+                to_line(c, d, line).wait_send()
+                from_line(c, d, line).wait_send()
+            up(c, d, rank).wait_send()
+            down(c, d, rank).wait_send()
+            forwarded(c, d, rank).wait_send()
+        for i in range(4):
+            near(c, i).wait_send()
+        for way in range(2):
+            far(c, way).wait_send()
 
 
 def attend_kernel(
@@ -389,6 +484,8 @@
     out_ref,
     kvsend,
     kvland,
+    vland,
+    qrows,
     csend,
     cland,
     k_send,
@@ -425,26 +522,46 @@
     kvland[rows_at(seq, count), :] = kvsend[seq]
     kv_out.arrived()
 
-    c_out = Exchange("seq", lambda t: csend.at[t], lambda s: cland.at[s], c_send, c_recv)
-
-    def attend(t):
-        kv = kvland[...]
-        scores = lax.dot_general(
-            q_ref[t], kv, (((1,), (1,)), ((), ())), preferred_element_type=F32
-        )
+    c_out = Exchange("seq", lambda t: csend.at[rows_at(t, q_ref.shape[1])], lambda s: cland.at[s], c_send, c_recv)
+
+    wide_lane = lax.broadcasted_iota(jnp.int32, kvland.shape, 1)
+    key_side = 64 * (1 - lax.rem(seq, 2))
+    is_key = (wide_lane >= key_side) & (wide_lane < key_side + 64)
+    vland[...] = jnp.where(is_key, jnp.ones((), BF16), kvland[...])
+    pair_rows = 2 * q_ref.shape[1]
+
+    def scores_of(i):
+        return lax.dot_general(
+            qrows[rows_at(i, pair_rows), :],
+            kvland[...],
+            (((1,), (1,)), ((), ())),
+            preferred_element_type=F32,
+        )
+
+    def context_of(scores):
         expo = jnp.exp(scores - jnp.max(scores, axis=-1, keepdims=True))
-        total = jnp.sum(expo, axis=-1, keepdims=True)
-        mixed = jnp.dot(expo.astype(BF16), kv, preferred_element_type=F32)
-        return (mixed / total).astype(BF16)
+        mixed = jnp.dot(expo.astype(BF16), vland[...], preferred_element_type=F32)
+        return (mixed / pltpu.roll(mixed, 64, 1)).astype(BF16)
+
+    qrows[...] = q_ref[...].reshape(qrows.shape)
+    group = 4
 
     def step(d, carry):
-        t = lax.rem(seq + d, n_seq)
-        csend[t] = attend(t)
-        c_out.start_one(d)
+        g = lax.rem(seq // group + d, n_seq // group)
+        both = [scores_of(2 * g + i) for i in range(2)]
+        for i in range(2):
+            csend[rows_at(2 * g + i, pair_rows), :] = context_of(both[i])
+        for i in range(group):
+            t = g * group + i
+
+            @pl.when(t != seq)
+            def _():
+                c_out.start_one(lax.rem(t - seq + n_seq, n_seq))
+
         return carry
 
-    lax.fori_loop(1, n_seq, step, 0)
-    cland[seq] = attend(seq)
+    lax.fori_loop(0, n_seq // group, step, 0)
+    cland[seq] = csend[rows_at(seq, q_ref.shape[1]), :]
     c_out.arrived()
     low = lax.broadcasted_iota(jnp.int32, cland.shape[1:], 1) < 64
     for p in range(HEADS // 2):
@@ -496,6 +613,8 @@
             pltpu.VMEM((experts, tok_rows, width), BF16),
             weight,
             weight,
+            pltpu.VMEM((part_ff, width), BF16),
+            pltpu.VMEM((experts, tok_rows, experts * part_ff), BF16),
             pltpu.VMEM((experts, tok_rows, width), F32),
             half,
             half,
@@ -508,12 +627,14 @@
             pltpu.VMEM((n_seq, q_rows, 128), BF16),
             dma((4,)),
         ]
-        + [dma((n_exp,))] * 4
+        + [dma((CHUNKS, n_exp))] * 4
         + [dma((n_seq,))] * 2
-        + [dma((experts,))] * 12
+        + [dma((experts,))] * 4
         + [dma((2,))] * 2
-        + [dma((4,))] * 2
-        + [dma((experts,))] * 2,
+        + [dma((CHUNKS, experts))] * 8
+        + [dma((CHUNKS, 2))] * 2
+        + [dma((CHUNKS, 4))] * 2
+        + [dma((CHUNKS, experts))] * 2,
         compiler_params=pltpu.CompilerParams(
             collective_id=0, has_side_effects=True, vmem_limit_bytes=56 << 20
         ),
@@ -544,7 +665,9 @@
         scratch_shapes=[
             pltpu.VMEM((n_seq, tok_rows, 128), BF16),
             pltpu.VMEM((n_seq * tok_rows, 128), BF16),
-            pltpu.VMEM((n_seq, q_rows, 128), BF16),
+            pltpu.VMEM((n_seq * tok_rows, 128), BF16),
+            pltpu.VMEM((n_seq * q_rows, 128), BF16),
+            pltpu.VMEM((n_seq * q_rows, 128), BF16),
             pltpu.VMEM((n_seq, q_rows, 128), BF16),
         ]
         + [dma((n_seq,))] * 4,

time: 132 us -> 140 us (1.061)
  Pallas kernels: 127 us -> 135 us
    pallas_call x1, Pallas kernels: 88.1 us -> 95.9 us  [per_device(): pl.pallas_call(moe_kernel, out_shape=(jax.ShapeDtypeStruct((tok_rows, wid...]
where the time goes in v3:
time: 140 us; the launch traced here: 139 us
  Pallas kernels  135 us (96%)
  matrix products  1.67 us (1%)
    pallas_call x1, Pallas kernels, per_device(): pl.pallas_call(moe_kernel, out_shape=(jax.ShapeDtypeStruct((tok_rows, wid...  95.9 us
    pallas_call x1, Pallas kernels, per_device(): pl.pallas_call(attend_kernel, out_shape=jax.ShapeDtypeStruct((q_rows, wid...  38.8 us

profile of v3, /device:TPU:2, one launch (start us, length us, event | category | flops | bytes accessed | tf_op | source)
XLA Modules:
  0.0 138.7 jit_solution(3768135653755277947)
XLA Ops:
  0.6 0.0 copy-start.4
  0.6 0.0 copy-start.6
  0.7 0.8 compare_select_fusion
  1.4 0.0 copy-start.5
  1.4 0.0 copy-start.1
  1.4 95.9 %experts.1 = (bf16[256,1024]{1,0:T(8,128)(2,1)}, bf16[16,128,128]{2,1,0:T(8,128)(2,1)}) custom-call(bf16[256,1024]{1,0:T(8,128)(2,1)} %bitcast.13, s32[1,256]{1,0:T(1,128)} %ids_ref.1, s32[1,256]{1,0:T(1,128)} %slots_ref.1, f32[1,1024]{1,0:T(1,128)} %bitcast.15, bf16[4,176,1024]{2,1,0:T(8,128)(2,1)} %bitcast.11, bf16[4,176,1024]{2,1,0:T(8,128)(2,1)} %wout_ref.1, ...), custom_call_target="tpu_custom_call" | custom-call | tf_op jit(solution)/shard_map/experts/pallas_call | solution.py:599
  97.3 0.0 copy-start
  97.3 0.0 copy-start.2
  97.3 0.0 copy-done.4
  97.3 0.0 copy-done.6
  97.3 1.7 %fusion.2 = (f32[256]{0:T(256)S(1)}, bf16[256,1024]{1,0:T(8,128)(2,1)S(1)}) fusion(bf16[256,1024]{1,0:T(8,128)(2,1)} %get-tuple-element.4, s32[256]{0:T(256)S(1)} %bitcast.16, f32[256]{0:T(256)S(1)} %bitcast.17, bf16[1,256,1024]{2,1,0:T(8,128)(2,1)S(1)} %copy-done.4), kind=kOutput, calls=%fused_computation.5 | convolution fusion | flops 136118016 | bytes 1575936 | tf_op jit(solution)/shard_map/dot_general | solution.py:656
  99.0 0.0 copy-start.3
  99.0 0.0 copy-done.5
  99.0 0.2 fusion.4.rows_ref
  99.2 0.0 copy-done.1
  99.2 0.0 copy-done
  99.3 0.0 copy-done.2
  99.3 38.8 %attend.1 = bf16[128,1024]{1,0:T(8,128)(2,1)S(1)} custom-call(bf16[256,1024]{1,0:T(8,128)(2,1)S(1)} %fusion.4.rows_ref, bf16[1024,1024]{1,0:T(8,128)(2,1)S(1)} %copy-done, bf16[1024,1024]{1,0:T(8,128)(2,1)S(1)} %copy-done.1, bf16[16,128,128]{2,1,0:T(8,128)(2,1)S(1)} %copy-done.2), custom_call_target="tpu_custom_call" | custom-call | tf_op jit(solution)/shard_map/attend/pallas_call | solution.py:660
  138.0 0.0 copy-done.3
  138.0 0.7 copy.14
  (1 shorter events, 0.0 us)
Async XLA Ops:
  0.6 96.7 %copy-start.4 = (bf16[1,256,1024]{2,1,0:T(8,128)(2,1)S(1)}, bf16[1,256,1024]{2,1,0:T(8,128)(2,1)}, u32[]{:S(2)}) copy-start(bf16[1,256,1024]{2,1,0:T(8,128)(2,1)} %param.11) | copy-start | bytes 1572868
  0.6 96.7 %copy-start.6 = (f32[1,256]{1,0:T(1,128)S(1)}, f32[1,256]{1,0:T(1,128)}, u32[]{:S(2)}) copy-start(f32[1,256]{1,0:T(1,128)} %param.14) | copy-start | bytes 3076
  1.4 97.6 %copy-start.5 = (f32[1024]{0:T(1024)S(1)}, f32[1024]{0:T(1024)}, u32[]{:S(2)}) copy-start(f32[1024]{0:T(1024)} %param.18) | copy-start | bytes 12292
  1.4 97.8 %copy-start.1 = (bf16[1024,1024]{1,0:T(8,128)(2,1)S(1)}, bf16[1024,1024]{1,0:T(8,128)(2,1)}, u32[]{:S(2)}) copy-start(bf16[1024,1024]{1,0:T(8,128)(2,1)} %wv_ref.1) | copy-start | bytes 6291460
  97.3 2.0 %copy-start = (bf16[1024,1024]{1,0:T(8,128)(2,1)S(1)}, bf16[1024,1024]{1,0:T(8,128)(2,1)}, u32[]{:S(2)}) copy-start(bf16[1024,1024]{1,0:T(8,128)(2,1)} %wk_ref.1) | copy-start | bytes 6291460
  97.3 2.0 %copy-start.2 = (bf16[16,128,128]{2,1,0:T(8,128)(2,1)S(1)}, bf16[16,128,128]{2,1,0:T(8,128)(2,1)}, u32[]{:S(2)}) copy-start(bf16[16,128,128]{2,1,0:T(8,128)(2,1)} %get-tuple-element.5.q_ref) | copy-start | bytes 1572868
  99.0 39.0 %copy-start.3 = (bf16[256,1024]{1,0:T(8,128)(2,1)}, bf16[256,1024]{1,0:T(8,128)(2,1)S(1)}, u32[]{:S(2)}) copy-start(bf16[256,1024]{1,0:T(8,128)(2,1)S(1)} %get-tuple-element.7) | copy-start | bytes 1572868

commit v4 on v3

--- a/solution.py
+++ b/solution.py
@@ -8,7 +8,8 @@
 from jax.sharding import PartitionSpec as P
 
 HEADS = 16
-CHUNKS = 2
+OUT_CHUNKS = 1
+BACK_CHUNKS = 2
 MESH = pl.DeviceIdType.MESH
 F32 = jnp.float32
 BF16 = jnp.bfloat16
@@ -77,7 +78,7 @@
     def arrived(self):
         self.loop(self.wait_one)
 
-    def sent(self):
+    def wait_send(self):
         self.loop(lambda d: self.copy(d, self.me).wait_send())
 
 
@@ -112,7 +113,12 @@
     wout_land,
     relay,
     hidden,
-    part,
+    far_part,
+    up_part,
+    down_part,
+    up_wait,
+    down_wait,
+    own_part,
     half_up,
     half_down,
     full_up,
@@ -187,13 +193,31 @@
     in_row = lax.broadcasted_iota(jnp.int32, (tok, tok), 1)
     dispatch = (out_row == target).astype(BF16)
     packed[...] = jnp.dot(dispatch, normed, preferred_element_type=F32).astype(BF16)
+    q_in.wait()
+    q_half = q_ref.shape[0] // 2
+    lane = lax.broadcasted_iota(jnp.int32, (q_half, 128), 1)
+    for p in range(HEADS // 2):
+        pair = query[:, p * 128 : (p + 1) * 128].astype(F32) * 0.125
+        turned = pltpu.roll(pair, 64, 1)
+        qsend[2 * p] = jnp.where(lane < 64, pair[:q_half], turned[q_half:]).astype(BF16)
+        qsend[2 * p + 1] = jnp.where(lane < 64, turned[:q_half], pair[q_half:]).astype(BF16)
     pl.semaphore_wait(barrier, greeted)
 
-    chunks = z_send.shape[0]
+    started = []
+
+    def go(transfer):
+        transfer.start()
+        started.append(transfer)
+
+    chunks, back_chunks = z_send.shape[0], b_send.shape[0]
     wide = enc_ref.shape[1] // chunks
+    back_wide = enc_ref.shape[1] // back_chunks
 
     def cols(c):
         return pl.ds(c * wide, wide)
+
+    def bcols(c):
+        return pl.ds(c * back_wide, back_wide)
 
     def z_out(c):
         return Exchange(
@@ -230,25 +254,19 @@
     w_first = (win_ref, win_land, wi_send, wi_recv)
     w_second = (wout_ref, wout_land, wo_send, wo_recv)
     direct = [(d, w_first) for d in range(1, experts)] + [(d, w_second) for d in (1, 3)]
-    z_out(0).start()
-    relay_in.start()
-    for d, each in direct:
-        weight_copy(d, line, *each).start()
-    for c in range(1, chunks):
-        z_out(c).start()
-    zland[rows_at(exp, zrows), :] = packed[rows_at(exp, zrows), :]
-
-    q_in.wait()
-    lane = lax.broadcasted_iota(jnp.int32, (q_ref.shape[0], 128), 1)
-    for p in range(HEADS // 2):
-        pair = pltpu.roll(query[:, p * 128 : (p + 1) * 128].astype(F32) * 0.125, 64, 1)
-        qsend[2 * p] = jnp.where(lane >= 64, pair, 0.0).astype(BF16)
-        qsend[2 * p + 1] = jnp.where(lane < 64, pair, 0.0).astype(BF16)
+    go(z_out(0))
     q_out = Exchange(
         "seq", lambda t: qsend.at[t], lambda s: qland_ref.at[s], q_send, q_recv
     )
     q_own = pltpu.make_async_copy(qsend.at[seq], qland_ref.at[seq], local_sem.at[0])
     q_own.start()
+    go(q_out)
+    go(relay_in)
+    for d, each in direct:
+        go(weight_copy(d, line, *each))
+    for c in range(1, chunks):
+        go(z_out(c))
+    zland[rows_at(exp, zrows), :] = packed[rows_at(exp, zrows), :]
 
     def by_expert(r):
         j, k, c = r // zrows, lax.rem(r // capacity, experts), lax.rem(r, capacity)
@@ -257,7 +275,7 @@
     forward = (by_expert(in_row) == out_row).astype(BF16)
     inverse = (by_expert(out_row) == in_row).astype(BF16)
     relay_in.wait_recv()
-    relay_out(turn(line, 1)).start()
+    go(relay_out(turn(line, 1)))
 
     above, below, across = turn(rank, 1), turn(rank, -1), turn(rank, 2)
 
@@ -307,19 +325,19 @@
             forward, zland[:, cols(c)], preferred_element_type=F32
         ).astype(BF16)
         for d in range(1, experts):
-            to_line(c, d, line).start()
+            go(to_line(c, d, line))
         rland[rank, rows_at(line, srows), cols(c)] = rows[rows_at(line, srows), cols(c)]
         for d in range(experts):
             if d:
                 to_line(c, d, turn(line, -d)).wait_recv()
-            up(c, d, rank).start()
-            down(c, d, rank).start()
+            go(up(c, d, rank))
+            go(down(c, d, rank))
         for d in (0, 1):
             up(c, d, below).wait_recv()
-            forwarded(c, d, below).start()
+            go(forwarded(c, d, below))
         for d in (2, 3):
             down(c, d, above).wait_recv()
-            forwarded(c, d, above).start()
+            go(forwarded(c, d, above))
 
     def first_layer(r):
         product = lax.dot_general(
@@ -356,23 +374,23 @@
     def far(c, way):
         half, land, r = ((first, half_up, above), (second, half_down, below))[way]
         return remote(
-            part.at[across, half, cols(c)],
-            land.at[:, cols(c)],
+            far_part.at[half, bcols(c)],
+            land.at[:, bcols(c)],
             h_send.at[c, way],
             h_recv.at[c, way],
             at(line, r),
         )
 
     def near(c, i):
-        r, half, land = (
-            (above, second, full_up),
-            (below, first, full_down),
-            (above, first, full_up),
-            (below, second, full_down),
+        r, half, source, land = (
+            (above, second, up_part, full_up),
+            (below, first, down_part, full_down),
+            (above, first, up_part, full_up),
+            (below, second, down_part, full_down),
         )[i]
         return remote(
-            part.at[r, half, cols(c)],
-            land.at[half, cols(c)],
+            source.at[half, bcols(c)],
+            land.at[half, bcols(c)],
             f_send.at[c, i],
             f_recv.at[c, i],
             at(line, r),
@@ -381,8 +399,8 @@
     def from_line(c, d, slot):
         g = turn(line, d)
         return remote(
-            brows.at[rows_at(g, srows), cols(c)],
-            gback.at[rows_at(slot, srows), cols(c)],
+            brows.at[rows_at(g, srows), bcols(c)],
+            gback.at[rows_at(slot, srows), bcols(c)],
             gb_send.at[c, d],
             gb_recv.at[c, d],
             at(g, rank),
@@ -391,89 +409,79 @@
     def b_out(c):
         return Exchange(
             "exp",
-            lambda t: zback.at[rows_at(t, zrows), cols(c)],
-            lambda s: bland.at[rows_at(s, zrows), cols(c)],
+            lambda t: zback.at[rows_at(t, zrows), bcols(c)],
+            lambda s: bland.at[rows_at(s, zrows), bcols(c)],
             b_send.at[c],
             b_recv.at[c],
         )
 
     def second_layer(c):
         def one(r):
-            part[r, :, cols(c)] = jnp.dot(
-                hidden[r], wout_land[:, cols(c)], preferred_element_type=F32
-            )
-
-        one(across)
-        far(c, 0).start()
-        far(c, 1).start()
-        one(above)
-        near(c, 0).start()
-        one(below)
-        near(c, 1).start()
-        one(rank)
+            return jnp.dot(hidden[r], wout_land[:, bcols(c)], preferred_element_type=F32)
+
+        far_part[:, bcols(c)] = one(across).astype(BF16)
+        go(far(c, 0))
+        go(far(c, 1))
+        product = one(above)
+        up_part[second, bcols(c)] = product[mid:].astype(BF16)
+        go(near(c, 0))
+        up_wait[:, bcols(c)] = product[:mid]
+        product = one(below)
+        down_part[first, bcols(c)] = product[:mid].astype(BF16)
+        go(near(c, 1))
+        down_wait[:, bcols(c)] = product[mid:]
+        own_part[:, bcols(c)] = one(rank)
 
     def add_far(c):
         far(c, 0).wait_recv()
-        part[above, first, cols(c)] = part[above, first, cols(c)] + half_up[:, cols(c)]
-        near(c, 2).start()
+        up_part[first, bcols(c)] = (
+            up_wait[:, bcols(c)] + half_up[:, bcols(c)].astype(F32)
+        ).astype(BF16)
+        go(near(c, 2))
         far(c, 1).wait_recv()
-        part[below, second, cols(c)] = part[below, second, cols(c)] + half_down[:, cols(c)]
-        near(c, 3).start()
+        down_part[second, bcols(c)] = (
+            down_wait[:, bcols(c)] + half_down[:, bcols(c)].astype(F32)
+        ).astype(BF16)
+        go(near(c, 3))
 
     def finish(c):
         for i in (0, 1, 2, 3):
             near(c, i).wait_recv()
-        brows[:, cols(c)] = (
-            part[rank, :, cols(c)] + full_up[:, cols(c)] + full_down[:, cols(c)]
+        brows[:, bcols(c)] = (
+            own_part[:, bcols(c)]
+            + full_up[:, bcols(c)].astype(F32)
+            + full_down[:, bcols(c)].astype(F32)
         ).astype(BF16)
         for d in range(1, experts):
-            from_line(c, d, line).start()
-        gback[rows_at(line, srows), cols(c)] = brows[rows_at(line, srows), cols(c)]
+            go(from_line(c, d, line))
+        gback[rows_at(line, srows), bcols(c)] = brows[rows_at(line, srows), bcols(c)]
 
     def give_back(c):
         for d in range(1, experts):
             from_line(c, d, turn(line, -d)).wait_recv()
-        zback[:, cols(c)] = jnp.dot(
-            inverse, gback[:, cols(c)], preferred_element_type=F32
+        zback[:, bcols(c)] = jnp.dot(
+            inverse, gback[:, bcols(c)], preferred_element_type=F32
         ).astype(BF16)
-        b_out(c).start()
-        bland[rows_at(exp, zrows), cols(c)] = zback[rows_at(exp, zrows), cols(c)]
+        go(b_out(c))
+        bland[rows_at(exp, zrows), bcols(c)] = zback[rows_at(exp, zrows), bcols(c)]
 
     second_layer(0)
     add_far(0)
-    for c in range(1, chunks):
+    for c in range(1, back_chunks):
         second_layer(c)
         finish(c - 1)
         add_far(c)
         give_back(c - 1)
-    finish(chunks - 1)
-    q_out.start()
-    give_back(chunks - 1)
+    finish(back_chunks - 1)
+    give_back(back_chunks - 1)
 
     q_own.wait()
     q_out.arrived()
-    for c in range(chunks):
+    for c in range(back_chunks):
         b_out(c).arrived()
     back_ref[...] = bland[...]
-    q_out.sent()
-    for d, each in direct:
-        weight_copy(d, line, *each).wait_send()
-    relay_in.wait_send()
-    relay_out(line).wait_send()
-    for c in range(chunks):
-        z_out(c).sent()
-        b_out(c).sent()
-        for d in range(experts):
-            if d:
-                to_line(c, d, line).wait_send()
-                from_line(c, d, line).wait_send()
-            up(c, d, rank).wait_send()
-            down(c, d, rank).wait_send()
-            forwarded(c, d, rank).wait_send()
-        for i in range(4):
-            near(c, i).wait_send()
-        for way in range(2):
-            far(c, way).wait_send()
+    for transfer in started:
+        transfer.wait_send()
 
 
 def attend_kernel(
@@ -520,15 +528,30 @@
     )
     kv_out.start()
     kvland[rows_at(seq, count), :] = kvsend[seq]
+
+    even = lax.rem(seq, 2) == 0
+    q_half = q_ref.shape[1]
+    q_count = 2 * q_half
+    packed = q_ref[...].reshape(n_seq * q_half, 128).astype(F32)
+    turned = pltpu.roll(packed, 64, 1)
+    side = lax.broadcasted_iota(jnp.int32, packed.shape, 1)
+    at_keys = jnp.where(even, side, side + 64) % 128 >= 64
+    top = jnp.where(at_keys, jnp.where(even, turned, packed), 0.0).astype(BF16)
+    bottom = jnp.where(at_keys, jnp.where(even, packed, turned), 0.0).astype(BF16)
+    for t in range(n_seq):
+        qrows[t * q_count : t * q_count + q_half, :] = top[t * q_half : (t + 1) * q_half]
+        qrows[t * q_count + q_half : (t + 1) * q_count, :] = bottom[t * q_half : (t + 1) * q_half]
     kv_out.arrived()
 
-    c_out = Exchange("seq", lambda t: csend.at[rows_at(t, q_ref.shape[1])], lambda s: cland.at[s], c_send, c_recv)
+    c_out = Exchange("seq", lambda t: csend.at[t], lambda s: cland.at[s], c_send, c_recv)
 
     wide_lane = lax.broadcasted_iota(jnp.int32, kvland.shape, 1)
     key_side = 64 * (1 - lax.rem(seq, 2))
     is_key = (wide_lane >= key_side) & (wide_lane < key_side + 64)
     vland[...] = jnp.where(is_key, jnp.ones((), BF16), kvland[...])
-    pair_rows = 2 * q_ref.shape[1]
+    pair_rows = 2 * q_count
+    lane = lax.broadcasted_iota(jnp.int32, (q_half, 128), 1)
+    at_values = jnp.where(even, lane, lane + 64) % 128 < 64
 
     def scores_of(i):
         return lax.dot_general(
@@ -541,16 +564,23 @@
     def context_of(scores):
         expo = jnp.exp(scores - jnp.max(scores, axis=-1, keepdims=True))
         mixed = jnp.dot(expo.astype(BF16), vland[...], preferred_element_type=F32)
-        return (mixed / pltpu.roll(mixed, 64, 1)).astype(BF16)
-
-    qrows[...] = q_ref[...].reshape(qrows.shape)
+        context = mixed / pltpu.roll(mixed, 64, 1)
+        turned = pltpu.roll(context, 64, 1)
+        return [
+            jnp.where(
+                at_values, context[i : i + q_half], turned[i + q_half : i + q_count]
+            ).astype(BF16)
+            for i in range(0, pair_rows, q_count)
+        ]
+
     group = 4
 
     def step(d, carry):
         g = lax.rem(seq // group + d, n_seq // group)
         both = [scores_of(2 * g + i) for i in range(2)]
         for i in range(2):
-            csend[rows_at(2 * g + i, pair_rows), :] = context_of(both[i])
+            for j, context in enumerate(context_of(both[i])):
+                csend[g * group + 2 * i + j] = context
         for i in range(group):
             t = g * group + i
 
@@ -561,13 +591,16 @@
         return carry
 
     lax.fori_loop(0, n_seq // group, step, 0)
-    cland[seq] = csend[rows_at(seq, q_ref.shape[1]), :]
+    cland[seq] = csend[seq]
     c_out.arrived()
-    low = lax.broadcasted_iota(jnp.int32, cland.shape[1:], 1) < 64
     for p in range(HEADS // 2):
-        out_ref[:, p * 128 : (p + 1) * 128] = jnp.where(low, cland[2 * p], cland[2 * p + 1])
-    kv_out.sent()
-    c_out.sent()
+        one, two = cland[2 * p].astype(F32), cland[2 * p + 1].astype(F32)
+        out_ref[:q_half, p * 128 : (p + 1) * 128] = jnp.where(lane < 64, one, two).astype(BF16)
+        out_ref[q_half:, p * 128 : (p + 1) * 128] = pltpu.roll(
+            jnp.where(lane < 64, two, one), 64, 1
+        ).astype(BF16)
+    kv_out.wait_send()
+    c_out.wait_send()
 
 
 def per_device(
@@ -593,14 +626,13 @@
     hbm = pl.BlockSpec(memory_space=pl.ANY)
     dma = pltpu.SemaphoreType.DMA
     whole = pltpu.VMEM((tok_rows, width), BF16)
-    half = pltpu.VMEM((tok_rows // 2, width), F32)
-    full = pltpu.VMEM((tok_rows, width), F32)
+    half = pltpu.VMEM((tok_rows // 2, width), BF16)
     weight = pltpu.VMEM((experts * part_ff, width), BF16)
     back, queries = pl.pallas_call(
         moe_kernel,
         out_shape=(
             jax.ShapeDtypeStruct((tok_rows, width), BF16),
-            jax.ShapeDtypeStruct((n_seq, q_rows, 128), BF16),
+            jax.ShapeDtypeStruct((n_seq, q_rows // 2, 128), BF16),
         ),
         in_specs=[hbm, vmem, vmem, vmem, hbm, hbm, hbm],
         out_specs=(vmem, hbm),
@@ -615,26 +647,32 @@
             weight,
             pltpu.VMEM((part_ff, width), BF16),
             pltpu.VMEM((experts, tok_rows, experts * part_ff), BF16),
-            pltpu.VMEM((experts, tok_rows, width), F32),
+            whole,
+            whole,
+            whole,
+            pltpu.VMEM((tok_rows // 2, width), F32),
+            pltpu.VMEM((tok_rows // 2, width), F32),
+            pltpu.VMEM((tok_rows, width), F32),
             half,
             half,
-            full,
-            full,
-            whole,
-            whole,
-            whole,
-            whole,
-            pltpu.VMEM((n_seq, q_rows, 128), BF16),
+            whole,
+            whole,
+            whole,
+            whole,
+            whole,
+            whole,
+            pltpu.VMEM((n_seq, q_rows // 2, 128), BF16),
             dma((4,)),
         ]
-        + [dma((CHUNKS, n_exp))] * 4
+        + [dma((OUT_CHUNKS, n_exp))] * 2
+        + [dma((BACK_CHUNKS, n_exp))] * 2
         + [dma((n_seq,))] * 2
         + [dma((experts,))] * 4
         + [dma((2,))] * 2
-        + [dma((CHUNKS, experts))] * 8
-        + [dma((CHUNKS, 2))] * 2
-        + [dma((CHUNKS, 4))] * 2
-        + [dma((CHUNKS, experts))] * 2,
+        + [dma((OUT_CHUNKS, experts))] * 8
+        + [dma((BACK_CHUNKS, 2))] * 2
+        + [dma((BACK_CHUNKS, 4))] * 2
+        + [dma((BACK_CHUNKS, experts))] * 2,
         compiler_params=pltpu.CompilerParams(
             collective_id=0, has_side_effects=True, vmem_limit_bytes=56 << 20
         ),
@@ -667,8 +705,8 @@
             pltpu.VMEM((n_seq * tok_rows, 128), BF16),
             pltpu.VMEM((n_seq * tok_rows, 128), BF16),
             pltpu.VMEM((n_seq * q_rows, 128), BF16),
-            pltpu.VMEM((n_seq * q_rows, 128), BF16),
-            pltpu.VMEM((n_seq, q_rows, 128), BF16),
+            pltpu.VMEM((n_seq, q_rows // 2, 128), BF16),
+            pltpu.VMEM((n_seq, q_rows // 2, 128), BF16),
         ]
         + [dma((n_seq,))] * 4,
         compiler_params=pltpu.CompilerParams(

time: 140 us -> 123 us (0.88)
  Pallas kernels: 135 us -> 118 us
    pallas_call x1, Pallas kernels: 95.9 us -> 81.3 us  [per_device(): pl.pallas_call(moe_kernel, out_shape=(jax.ShapeDtypeStruct((tok_rows, wid...]
    pallas_call x1, Pallas kernels: 38.8 us -> 37.2 us  [per_device(): pl.pallas_call(attend_kernel, out_shape=jax.ShapeDtypeStruct((q_rows, wid...]
where the time goes in v4:
time: 123 us
  Pallas kernels  118 us (96%)
  matrix products  1.67 us (1%)
    pallas_call x1, Pallas kernels, per_device(): pl.pallas_call(moe_kernel, out_shape=(jax.ShapeDtypeStruct((tok_rows, wid...  81.3 us
    pallas_call x1, Pallas kernels, per_device(): pl.pallas_call(attend_kernel, out_shape=jax.ShapeDtypeStruct((q_rows, wid...  37.2 us

profile of v4, /device:TPU:2, one launch (start us, length us, event | category | flops | bytes accessed | tf_op | source)
XLA Modules:
  0.0 122.6 jit_solution(16001699997527332193)
XLA Ops:
  0.6 0.0 copy-start.4
  0.6 0.0 copy-start.6
  0.7 0.8 compare_select_fusion
  1.4 0.0 copy-start.5
  1.4 0.0 copy-start.1
  1.4 81.3 %experts.1 = (bf16[256,1024]{1,0:T(8,128)(2,1)}, bf16[16,64,128]{2,1,0:T(8,128)(2,1)}) custom-call(bf16[256,1024]{1,0:T(8,128)(2,1)} %bitcast.13, s32[1,256]{1,0:T(1,128)} %ids_ref.1, s32[1,256]{1,0:T(1,128)} %slots_ref.1, f32[1,1024]{1,0:T(1,128)} %bitcast.15, bf16[4,176,1024]{2,1,0:T(8,128)(2,1)} %bitcast.11, bf16[4,176,1024]{2,1,0:T(8,128)(2,1)} %wout_ref.1, ...), custom_call_target="tpu_custom_call" | custom-call | tf_op jit(solution)/shard_map/experts/pallas_call | solution.py:631
  82.7 0.0 copy-start
  82.7 0.0 copy-start.2
  82.7 0.0 copy-done.4
  82.8 0.0 copy-done.6
  82.8 1.7 %fusion.2 = (f32[256]{0:T(256)S(1)}, bf16[256,1024]{1,0:T(8,128)(2,1)S(1)}) fusion(bf16[256,1024]{1,0:T(8,128)(2,1)} %get-tuple-element.4, s32[256]{0:T(256)S(1)} %bitcast.16, f32[256]{0:T(256)S(1)} %bitcast.17, bf16[1,256,1024]{2,1,0:T(8,128)(2,1)S(1)} %copy-done.4), kind=kOutput, calls=%fused_computation.5 | convolution fusion | flops 136118016 | bytes 1575936 | tf_op jit(solution)/shard_map/dot_general | solution.py:694
  84.4 0.0 copy-start.3
  84.5 0.0 copy-done.5
  84.5 0.2 fusion.4.rows_ref
  84.7 0.0 copy-done.1
  84.7 0.0 copy-done
  84.7 0.0 copy-done.2
  84.7 37.2 %attend.1 = bf16[128,1024]{1,0:T(8,128)(2,1)S(1)} custom-call(bf16[256,1024]{1,0:T(8,128)(2,1)S(1)} %fusion.4.rows_ref, bf16[1024,1024]{1,0:T(8,128)(2,1)S(1)} %copy-done, bf16[1024,1024]{1,0:T(8,128)(2,1)S(1)} %copy-done.1, bf16[16,64,128]{2,1,0:T(8,128)(2,1)S(1)} %copy-done.2), custom_call_target="tpu_custom_call" | custom-call | tf_op jit(solution)/shard_map/attend/pallas_call | solution.py:698
  121.9 0.0 copy-done.3
  121.9 0.7 copy.14
  (1 shorter events, 0.0 us)
Async XLA Ops:
  0.6 82.1 %copy-start.4 = (bf16[1,256,1024]{2,1,0:T(8,128)(2,1)S(1)}, bf16[1,256,1024]{2,1,0:T(8,128)(2,1)}, u32[]{:S(2)}) copy-start(bf16[1,256,1024]{2,1,0:T(8,128)(2,1)} %param.11) | copy-start | bytes 1572868
  0.6 82.1 %copy-start.6 = (f32[1,256]{1,0:T(1,128)S(1)}, f32[1,256]{1,0:T(1,128)}, u32[]{:S(2)}) copy-start(f32[1,256]{1,0:T(1,128)} %param.14) | copy-start | bytes 3076
  1.4 83.0 %copy-start.5 = (f32[1024]{0:T(1024)S(1)}, f32[1024]{0:T(1024)}, u32[]{:S(2)}) copy-start(f32[1024]{0:T(1024)} %param.18) | copy-start | bytes 12292
  1.4 83.3 %copy-start.1 = (bf16[1024,1024]{1,0:T(8,128)(2,1)S(1)}, bf16[1024,1024]{1,0:T(8,128)(2,1)}, u32[]{:S(2)}) copy-start(bf16[1024,1024]{1,0:T(8,128)(2,1)} %wv_ref.1) | copy-start | bytes 6291460
  82.7 2.0 %copy-start = (bf16[1024,1024]{1,0:T(8,128)(2,1)S(1)}, bf16[1024,1024]{1,0:T(8,128)(2,1)}, u32[]{:S(2)}) copy-start(bf16[1024,1024]{1,0:T(8,128)(2,1)} %wk_ref.1) | copy-start | bytes 6291460
  82.7 2.0 %copy-start.2 = (bf16[16,64,128]{2,1,0:T(8,128)(2,1)S(1)}, bf16[16,64,128]{2,1,0:T(8,128)(2,1)}, u32[]{:S(2)}) copy-start(bf16[16,64,128]{2,1,0:T(8,128)(2,1)} %get-tuple-element.5.q_ref) | copy-start | bytes 786436
  84.4 37.5 %copy-start.3 = (bf16[256,1024]{1,0:T(8,128)(2,1)}, bf16[256,1024]{1,0:T(8,128)(2,1)S(1)}, u32[]{:S(2)}) copy-start(bf16[256,1024]{1,0:T(8,128)(2,1)S(1)} %get-tuple-element.7) | copy-start | bytes 1572868

commit v5 on v4

--- a/solution.py
+++ b/solution.py
@@ -10,6 +10,7 @@
 HEADS = 16
 OUT_CHUNKS = 1
 BACK_CHUNKS = 2
+KEY_GROUPS = 2
 MESH = pl.DeviceIdType.MESH
 F32 = jnp.float32
 BF16 = jnp.bfloat16
@@ -43,7 +44,8 @@
 
 
 class Exchange:
-    def __init__(self, axis, source, landing, send, recv):
+    def __init__(self, axis, source, landing, send, recv, by_step=False):
+        self.by_step = by_step
         self.axis, self.source, self.landing = axis, source, landing
         self.send, self.recv = send, recv
         self.n, self.me = lax.axis_size(axis), lax.axis_index(axis)
@@ -60,23 +62,24 @@
         )
 
     def start_one(self, d):
-        self.copy(d, self.me).start()
+        self.copy(d, d if self.by_step else self.me).start()
 
     def wait_one(self, d):
-        self.copy(d, lax.rem(self.me + self.n - d, self.n)).wait_recv()
-
-    def loop(self, act):
+        slot = d if self.by_step else lax.rem(self.me + self.n - d, self.n)
+        self.copy(d, slot).wait_recv()
+
+    def loop(self, act, first=1, last=None):
         def body(d, carry):
             act(d)
             return carry
 
-        lax.fori_loop(1, self.n, body, 0)
+        lax.fori_loop(first, self.n if last is None else last, body, 0)
 
     def start(self):
         self.loop(self.start_one)
 
-    def arrived(self):
-        self.loop(self.wait_one)
+    def arrived(self, first=1, last=None):
+        self.loop(self.wait_one, first, last)
 
     def wait_send(self):
         self.loop(lambda d: self.copy(d, self.me).wait_send())
@@ -93,25 +96,31 @@
     )
 
 
-def moe_kernel(
+def layer_kernel(
     enc_ref,
     ids_ref,
     slots_ref,
+    gate_ref,
     gain_ref,
     win_ref,
     wout_ref,
+    final_gain_ref,
+    wk_ref,
+    wv_ref,
     q_ref,
-    back_ref,
-    qland_ref,
+    enc_out_ref,
+    out_ref,
     enc,
     query,
+    place,
+    w_key,
+    w_value,
     packed,
     zland,
     rows,
     rland,
     win_land,
     wout_land,
-    relay,
     hidden,
     far_part,
     up_part,
@@ -128,6 +137,15 @@
     zback,
     bland,
     qsend,
+    qland,
+    qrows,
+    kvsend,
+    kvland,
+    vland,
+    sums,
+    peaks,
+    csend,
+    cland,
     local_sem,
     z_send,
     z_recv,
@@ -139,8 +157,6 @@
     wi_recv,
     wo_send,
     wo_recv,
-    relay_send,
-    relay_recv,
     g_send,
     g_recv,
     up_send,
@@ -155,6 +171,10 @@
     f_recv,
     gb_send,
     gb_recv,
+    k_send,
+    k_recv,
+    c_send,
+    c_recv,
 ):
     seq, exp = lax.axis_index("seq"), lax.axis_index("exp")
     n_seq, n_exp = lax.axis_size("seq"), lax.axis_size("exp")
@@ -178,6 +198,10 @@
     enc_in.start()
     q_in.start()
     barrier, greeted = signal_all(("seq", "exp"))
+    projections = [
+        pltpu.make_async_copy(ref, land, local_sem.at[4 + i])
+        for i, (ref, land) in enumerate(((wk_ref, w_key), (wv_ref, w_value)))
+    ]
     own_weights = [
         pltpu.make_async_copy(
             ref.at[line], land.at[rows_at(line, hidden_part)], local_sem.at[2 + i]
@@ -191,8 +215,8 @@
     target = jnp.where(slots_ref[...] < capacity, ids_ref[...] * capacity + slots_ref[...], -1)
     out_row = lax.broadcasted_iota(jnp.int32, (tok, tok), 0)
     in_row = lax.broadcasted_iota(jnp.int32, (tok, tok), 1)
-    dispatch = (out_row == target).astype(BF16)
-    packed[...] = jnp.dot(dispatch, normed, preferred_element_type=F32).astype(BF16)
+    place[...] = (out_row == target).astype(BF16)
+    packed[...] = jnp.dot(place[...], normed, preferred_element_type=F32).astype(BF16)
     q_in.wait()
     q_half = q_ref.shape[0] // 2
     lane = lax.broadcasted_iota(jnp.int32, (q_half, 128), 1)
@@ -234,38 +258,16 @@
             ref.at[k], land.at[rows_at(slot, hidden_part)], send.at[d], recv.at[d], at(k, rank)
         )
 
-    relay_in = remote(
-        wout_ref.at[turn(line, 2)],
-        relay,
-        relay_send.at[0],
-        relay_recv.at[0],
-        at(turn(line, -1), rank),
-    )
-
-    def relay_out(slot):
-        return remote(
-            relay,
-            wout_land.at[rows_at(slot, hidden_part)],
-            relay_send.at[1],
-            relay_recv.at[1],
-            at(turn(line, -1), rank),
-        )
-
     w_first = (win_ref, win_land, wi_send, wi_recv)
     w_second = (wout_ref, wout_land, wo_send, wo_recv)
-    direct = [(d, w_first) for d in range(1, experts)] + [(d, w_second) for d in (1, 3)]
+    direct = [(d, w_first) for d in range(1, experts)] + [(d, w_second) for d in range(1, experts)]
     go(z_out(0))
-    q_out = Exchange(
-        "seq", lambda t: qsend.at[t], lambda s: qland_ref.at[s], q_send, q_recv
-    )
-    q_own = pltpu.make_async_copy(qsend.at[seq], qland_ref.at[seq], local_sem.at[0])
-    q_own.start()
-    go(q_out)
-    go(relay_in)
     for d, each in direct:
         go(weight_copy(d, line, *each))
     for c in range(1, chunks):
         go(z_out(c))
+    for copy in projections:
+        copy.start()
     zland[rows_at(exp, zrows), :] = packed[rows_at(exp, zrows), :]
 
     def by_expert(r):
@@ -274,8 +276,6 @@
 
     forward = (by_expert(in_row) == out_row).astype(BF16)
     inverse = (by_expert(out_row) == in_row).astype(BF16)
-    relay_in.wait_recv()
-    go(relay_out(turn(line, 1)))
 
     above, below, across = turn(rank, 1), turn(rank, -1), turn(rank, 2)
 
@@ -366,7 +366,6 @@
     for d, each in direct:
         if each is w_second:
             weight_copy(d, turn(line, -d), *each).wait_recv()
-    relay_out(turn(line, 2)).wait_recv()
 
     mid = tok // 2
     first, second = pl.ds(0, mid), pl.ds(mid, mid)
@@ -475,44 +474,29 @@
     finish(back_chunks - 1)
     give_back(back_chunks - 1)
 
-    q_own.wait()
-    q_out.arrived()
+    q_out = Exchange(
+        "seq", lambda t: qsend.at[t], lambda s: qland.at[s], q_send, q_recv
+    )
+    go(q_out)
+    qland[seq] = qsend[seq]
+
+    diagonal = out_row == in_row
+    gate = jnp.sum(jnp.where(diagonal, gate_ref[...], 0.0), axis=1, keepdims=True)
     for c in range(back_chunks):
         b_out(c).arrived()
-    back_ref[...] = bland[...]
-    for transfer in started:
-        transfer.wait_send()
-
-
-def attend_kernel(
-    rows_ref,
-    wk_ref,
-    wv_ref,
-    q_ref,
-    out_ref,
-    kvsend,
-    kvland,
-    vland,
-    qrows,
-    csend,
-    cland,
-    k_send,
-    k_recv,
-    c_send,
-    c_recv,
-):
-    seq = lax.axis_index("seq")
-    n_seq = lax.axis_size("seq")
-    count = rows_ref.shape[0]
-    barrier, greeted = signal_all(("seq",))
-    pl.semaphore_wait(barrier, greeted)
-    lane = lax.broadcasted_iota(jnp.int32, (count, 128), 1)
+        combined = lax.dot_general(
+            place[...], bland[:, bcols(c)], (((0,), (0,)), ((), ())), preferred_element_type=F32
+        )
+        enc_out_ref[:, bcols(c)] = (enc[:, bcols(c)].astype(F32) + gate * combined).astype(BF16)
+    block = rms_scale(enc_out_ref[...].astype(F32), final_gain_ref[...]).astype(BF16)
+    for copy in projections:
+        copy.wait()
+    lane = lax.broadcasted_iota(jnp.int32, (tok, 128), 1)
     low = lane < 64
-    block = rows_ref[...]
     for g in range(HEADS // 4):
-        cols = slice(g * 256, (g + 1) * 256)
-        keys = jnp.dot(block, wk_ref[:, cols], preferred_element_type=F32)
-        values = jnp.dot(block, wv_ref[:, cols], preferred_element_type=F32)
+        span = slice(g * 256, (g + 1) * 256)
+        keys = jnp.dot(block, w_key[:, span], preferred_element_type=F32)
+        values = jnp.dot(block, w_value[:, span], preferred_element_type=F32)
         for i in range(2):
             k_pair = pltpu.roll(keys[:, i * 128 : (i + 1) * 128], 64, 1)
             v_pair = values[:, i * 128 : (i + 1) * 128]
@@ -522,75 +506,89 @@
     kv_out = Exchange(
         "seq",
         lambda t: kvsend.at[t],
-        lambda s: kvland.at[rows_at(s, count)],
+        lambda s: kvland.at[rows_at(s, tok)],
         k_send,
         k_recv,
+        by_step=True,
     )
-    kv_out.start()
-    kvland[rows_at(seq, count), :] = kvsend[seq]
-
+    go(kv_out)
+    kvland[0:tok, :] = kvsend[seq]
+
+    q_out.arrived()
     even = lax.rem(seq, 2) == 0
-    q_half = q_ref.shape[1]
     q_count = 2 * q_half
-    packed = q_ref[...].reshape(n_seq * q_half, 128).astype(F32)
-    turned = pltpu.roll(packed, 64, 1)
-    side = lax.broadcasted_iota(jnp.int32, packed.shape, 1)
+    folded = qland[...].reshape(n_seq * q_half, 128).astype(F32)
+    turned = pltpu.roll(folded, 64, 1)
+    side = lax.broadcasted_iota(jnp.int32, folded.shape, 1)
     at_keys = jnp.where(even, side, side + 64) % 128 >= 64
-    top = jnp.where(at_keys, jnp.where(even, turned, packed), 0.0).astype(BF16)
-    bottom = jnp.where(at_keys, jnp.where(even, packed, turned), 0.0).astype(BF16)
+    top = jnp.where(at_keys, jnp.where(even, turned, folded), 0.0).astype(BF16)
+    bottom = jnp.where(at_keys, jnp.where(even, folded, turned), 0.0).astype(BF16)
     for t in range(n_seq):
         qrows[t * q_count : t * q_count + q_half, :] = top[t * q_half : (t + 1) * q_half]
         qrows[t * q_count + q_half : (t + 1) * q_count, :] = bottom[t * q_half : (t + 1) * q_half]
-    kv_out.arrived()
 
     c_out = Exchange("seq", lambda t: csend.at[t], lambda s: cland.at[s], c_send, c_recv)
-
-    wide_lane = lax.broadcasted_iota(jnp.int32, kvland.shape, 1)
-    key_side = 64 * (1 - lax.rem(seq, 2))
-    is_key = (wide_lane >= key_side) & (wide_lane < key_side + 64)
-    vland[...] = jnp.where(is_key, jnp.ones((), BF16), kvland[...])
+    span_rows = kvland.shape[0] // KEY_GROUPS
+    wide_lane = lax.broadcasted_iota(jnp.int32, (span_rows, 128), 1)
+    is_key = jnp.where(even, wide_lane, wide_lane + 64) % 128 >= 64
     pair_rows = 2 * q_count
     lane = lax.broadcasted_iota(jnp.int32, (q_half, 128), 1)
     at_values = jnp.where(even, lane, lane + 64) % 128 < 64
-
-    def scores_of(i):
-        return lax.dot_general(
-            qrows[rows_at(i, pair_rows), :],
-            kvland[...],
-            (((1,), (1,)), ((), ())),
-            preferred_element_type=F32,
-        )
-
-    def context_of(scores):
-        expo = jnp.exp(scores - jnp.max(scores, axis=-1, keepdims=True))
-        mixed = jnp.dot(expo.astype(BF16), vland[...], preferred_element_type=F32)
-        context = mixed / pltpu.roll(mixed, 64, 1)
-        turned = pltpu.roll(context, 64, 1)
-        return [
-            jnp.where(
-                at_values, context[i : i + q_half], turned[i + q_half : i + q_count]
-            ).astype(BF16)
-            for i in range(0, pair_rows, q_count)
-        ]
-
     group = 4
 
-    def step(d, carry):
-        g = lax.rem(seq // group + d, n_seq // group)
-        both = [scores_of(2 * g + i) for i in range(2)]
-        for i in range(2):
-            for j, context in enumerate(context_of(both[i])):
-                csend[g * group + 2 * i + j] = context
-        for i in range(group):
-            t = g * group + i
-
-            @pl.when(t != seq)
-            def _():
-                c_out.start_one(lax.rem(t - seq + n_seq, n_seq))
-
-        return carry
-
-    lax.fori_loop(0, n_seq // group, step, 0)
+    def attend(part, last):
+        span = slice(part * span_rows, (part + 1) * span_rows)
+        per = span_rows // tok
+        kv_out.arrived(max(1, part * per), (part + 1) * per)
+        vland[span, :] = jnp.where(is_key, jnp.ones((), BF16), kvland[span, :])
+
+        def step(d, carry):
+            g = lax.rem(seq // group + d, n_seq // group)
+            tiles = [rows_at(2 * g + i, pair_rows) for i in range(2)]
+            both = [
+                lax.dot_general(
+                    qrows[tile, :],
+                    kvland[span, :],
+                    (((1,), (1,)), ((), ())),
+                    preferred_element_type=F32,
+                )
+                for tile in tiles
+            ]
+            for i, tile in enumerate(tiles):
+                peak = jnp.max(both[i], axis=-1, keepdims=True)
+                if part:
+                    old = peaks[tile, 0:1]
+                    peak = jnp.maximum(peak, old)
+                expo = jnp.exp(both[i] - peak).astype(BF16)
+                mixed = jnp.dot(expo, vland[span, :], preferred_element_type=F32)
+                if part:
+                    mixed = mixed + jnp.exp(old - peak) * sums[tile, :]
+                if not last:
+                    sums[tile, :] = mixed
+                    peaks[tile, :] = jnp.broadcast_to(peak, mixed.shape)
+                    continue
+                context = mixed / pltpu.roll(mixed, 64, 1)
+                turned = pltpu.roll(context, 64, 1)
+                for j in range(2):
+                    k = j * q_count
+                    csend[g * group + 2 * i + j] = jnp.where(
+                        at_values, context[k : k + q_half], turned[k + q_half : k + q_count]
+                    ).astype(BF16)
+            if last:
+                for i in range(group):
+                    t = g * group + i
+
+                    @pl.when(t != seq)
+                    def _():
+                        c_out.start_one(lax.rem(t - seq + n_seq, n_seq))
+
+            return carry
+
+        lax.fori_loop(0, n_seq // group, step, 0)
+
+    for part in range(KEY_GROUPS):
+        attend(part, part == KEY_GROUPS - 1)
+    started.append(c_out)
     cland[seq] = csend[seq]
     c_out.arrived()
     for p in range(HEADS // 2):
@@ -599,8 +597,8 @@
         out_ref[q_half:, p * 128 : (p + 1) * 128] = pltpu.roll(
             jnp.where(lane < 64, two, one), 64, 1
         ).astype(BF16)
-    kv_out.wait_send()
-    c_out.wait_send()
+    for transfer in started:
+        transfer.wait_send()
 
 
 def per_device(
@@ -619,7 +617,6 @@
     n_exp, n_seq = lax.axis_size("exp"), lax.axis_size("seq")
     tok_rows, width = enc_in.shape[1:]
     experts, _, part_ff = w_in.shape
-    capacity = tok_rows // (experts * n_exp)
     q_rows = dec_query.shape[1]
 
     vmem = pl.BlockSpec(memory_space=pltpu.VMEM)
@@ -628,24 +625,28 @@
     whole = pltpu.VMEM((tok_rows, width), BF16)
     half = pltpu.VMEM((tok_rows // 2, width), BF16)
     weight = pltpu.VMEM((experts * part_ff, width), BF16)
-    back, queries = pl.pallas_call(
-        moe_kernel,
+    square = pltpu.VMEM((width, width), BF16)
+    folded = pltpu.VMEM((n_seq, q_rows // 2, 128), BF16)
+    enc_out, context = pl.pallas_call(
+        layer_kernel,
         out_shape=(
             jax.ShapeDtypeStruct((tok_rows, width), BF16),
-            jax.ShapeDtypeStruct((n_seq, q_rows // 2, 128), BF16),
+            jax.ShapeDtypeStruct((q_rows, width), BF16),
         ),
-        in_specs=[hbm, vmem, vmem, vmem, hbm, hbm, hbm],
-        out_specs=(vmem, hbm),
+        in_specs=[hbm, vmem, vmem, vmem, vmem, hbm, hbm, vmem, hbm, hbm, hbm],
+        out_specs=(vmem, vmem),
         scratch_shapes=[
             whole,
             pltpu.VMEM((q_rows, width), BF16),
+            pltpu.VMEM((tok_rows, tok_rows), BF16),
+            square,
+            square,
             whole,
             whole,
             whole,
             pltpu.VMEM((experts, tok_rows, width), BF16),
             weight,
             weight,
-            pltpu.VMEM((part_ff, width), BF16),
             pltpu.VMEM((experts, tok_rows, experts * part_ff), BF16),
             whole,
             whole,
@@ -661,59 +662,44 @@
             whole,
             whole,
             whole,
-            pltpu.VMEM((n_seq, q_rows // 2, 128), BF16),
-            dma((4,)),
+            folded,
+            folded,
+            pltpu.VMEM((n_seq * q_rows, 128), BF16),
+            pltpu.VMEM((n_seq, tok_rows, 128), BF16),
+            pltpu.VMEM((n_seq * tok_rows, 128), BF16),
+            pltpu.VMEM((n_seq * tok_rows, 128), BF16),
+            pltpu.VMEM((n_seq * q_rows, 128), F32),
+            pltpu.VMEM((n_seq * q_rows, 128), F32),
+            folded,
+            folded,
+            dma((6,)),
         ]
         + [dma((OUT_CHUNKS, n_exp))] * 2
         + [dma((BACK_CHUNKS, n_exp))] * 2
         + [dma((n_seq,))] * 2
         + [dma((experts,))] * 4
-        + [dma((2,))] * 2
         + [dma((OUT_CHUNKS, experts))] * 8
         + [dma((BACK_CHUNKS, 2))] * 2
         + [dma((BACK_CHUNKS, 4))] * 2
-        + [dma((BACK_CHUNKS, experts))] * 2,
+        + [dma((BACK_CHUNKS, experts))] * 2
+        + [dma((n_seq,))] * 4,
         compiler_params=pltpu.CompilerParams(
             collective_id=0, has_side_effects=True, vmem_limit_bytes=56 << 20
         ),
-        name="experts",
+        name="layer",
     )(
         enc_in[0],
         expert_ids,
         slots,
+        expert_gate,
         moe_gain[None],
         jnp.swapaxes(w_in, 1, 2),
         w_out,
+        final_gain[None],
+        w_key,
+        w_value,
         dec_query[0],
     )
-
-    inputs = enc_in[0].astype(F32)
-    places = jnp.arange(tok_rows, dtype=jnp.int32)
-    target = jnp.where(slots[0] < capacity, expert_ids[0] * capacity + slots[0], -1)
-    combine = (target[:, None] == places[None, :]).astype(BF16)
-    combined = jnp.dot(combine, back, preferred_element_type=F32)
-    enc_rows = inputs + expert_gate[0][:, None] * combined
-    enc_out = enc_rows.astype(BF16)
-    kv_rows = rms_scale(enc_out.astype(F32), final_gain).astype(BF16)
-    context = pl.pallas_call(
-        attend_kernel,
-        out_shape=jax.ShapeDtypeStruct((q_rows, width), BF16),
-        in_specs=[vmem] * 4,
-        out_specs=vmem,
-        scratch_shapes=[
-            pltpu.VMEM((n_seq, tok_rows, 128), BF16),
-            pltpu.VMEM((n_seq * tok_rows, 128), BF16),
-            pltpu.VMEM((n_seq * tok_rows, 128), BF16),
-            pltpu.VMEM((n_seq * q_rows, 128), BF16),
-            pltpu.VMEM((n_seq, q_rows // 2, 128), BF16),
-            pltpu.VMEM((n_seq, q_rows // 2, 128), BF16),
-        ]
-        + [dma((n_seq,))] * 4,
-        compiler_params=pltpu.CompilerParams(
-            collective_id=1, has_side_effects=True, vmem_limit_bytes=40 << 20
-        ),
-        name="attend",
-    )(kv_rows, w_key, w_value, queries)
     return (enc_out[None], context[None])
 
 

time: 123 us -> 113 us (0.919)
  Pallas kernels: 118 us -> 108 us
  local copies, waits for them, and re-layouts: 0.74 us -> 3.54 us
  matrix products: 1.67 us -> 0 us
    pallas_call x2 -> x1, Pallas kernels: 118 us -> 108 us  [per_device(): pl.pallas_call(layer_kernel, out_shape=(jax.ShapeDtypeStruct((tok_rows, w...]
    unnamed x15 -> x2, local copies, waits for them, and re-layouts: 0.74 us -> 3.54 us
    dot_general x1 -> x0, matrix products: 1.67 us -> none  [per_device(): combined = jnp.dot(combine, back, preferred_element_type=F32)]
where the time goes in v5:
time: 113 us; the launch traced here: 112 us
  Pallas kernels  108 us (96%)
  local copies, waits for them, and re-layouts  3.54 us (3%)
    pallas_call x1, Pallas kernels, per_device(): pl.pallas_call(layer_kernel, out_shape=(jax.ShapeDtypeStruct((tok_rows, w...  108 us
    unnamed x2, local copies, waits for them, and re-layouts  3.54 us

profile of v5, /device:TPU:2, one launch (start us, length us, event | category | flops | bytes accessed | tf_op | source)
XLA Modules:
  0.0 112.5 jit_solution(15922991795558360948)
XLA Ops:
  0.6 108.3 %layer.1 = (bf16[256,1024]{1,0:T(8,128)(2,1)}, bf16[128,1024]{1,0:T(8,128)(2,1)}) custom-call(bf16[256,1024]{1,0:T(8,128)(2,1)} %bitcast.9, s32[1,256]{1,0:T(1,128)} %ids_ref.1, s32[1,256]{1,0:T(1,128)} %slots_ref.1, f32[1,256]{1,0:T(1,128)} %gate_ref.1, f32[1,1024]{1,0:T(1,128)} %bitcast.12, bf16[4,176,1024]{2,1,0:T(8,128)(2,1)} %bitcast.7, ...), custom_call_target="tpu_custom_call" | custom-call | tf_op jit(solution)/shard_map/layer/pallas_call | solution.py:630
  108.9 1.9 %copy.15 = bf16[1,256,1024]{2,1,0:T(8,128)(2,1)} copy(bf16[1,256,1024]{2,1,0:T(8,128)(2,1)} %bitcast.8) | data formatting | bytes 1048576
  110.8 1.7 %copy.16 = bf16[1,128,1024]{2,1,0:T(8,128)(2,1)} copy(bf16[1,128,1024]{2,1,0:T(8,128)(2,1)} %bitcast.11) | data formatting | bytes 524288

commit v6 on v5

--- a/solution.py
+++ b/solution.py
@@ -44,14 +44,14 @@
 
 
 class Exchange:
-    def __init__(self, axis, source, landing, send, recv, by_step=False):
-        self.by_step = by_step
+    def __init__(self, axis, source, landing, send, recv, route=None):
+        self.route, self.by_step = route, route is not None
         self.axis, self.source, self.landing = axis, source, landing
         self.send, self.recv = send, recv
         self.n, self.me = lax.axis_size(axis), lax.axis_index(axis)
 
     def copy(self, d, slot):
-        t = lax.rem(self.me + d, self.n)
+        t = self.route(d) if self.route else lax.rem(self.me + d, self.n)
         return pltpu.make_async_remote_copy(
             src_ref=self.source(t),
             dst_ref=self.landing(slot),
@@ -75,11 +75,14 @@
 
         lax.fori_loop(first, self.n if last is None else last, body, 0)
 
-    def start(self):
-        self.loop(self.start_one)
+    def start(self, first=1, last=None):
+        self.loop(self.start_one, first, last)
 
     def arrived(self, first=1, last=None):
         self.loop(self.wait_one, first, last)
+
+    def send_one(self, d):
+        self.copy(d, self.me).wait_send()
 
     def wait_send(self):
         self.loop(lambda d: self.copy(d, self.me).wait_send())
@@ -509,9 +512,10 @@
         lambda s: kvland.at[rows_at(s, tok)],
         k_send,
         k_recv,
-        by_step=True,
+        route=lambda d: at(turn(line, d // experts), turn(rank, lax.rem(d, experts))),
     )
-    go(kv_out)
+    per = n_seq // KEY_GROUPS
+    kv_out.start(1, per)
     kvland[0:tok, :] = kvsend[seq]
 
     q_out.arrived()
@@ -527,6 +531,8 @@
         qrows[t * q_count : t * q_count + q_half, :] = top[t * q_half : (t + 1) * q_half]
         qrows[t * q_count + q_half : (t + 1) * q_count, :] = bottom[t * q_half : (t + 1) * q_half]
 
+    kv_out.loop(kv_out.send_one, 1, per)
+    kv_out.start(per, n_seq)
     c_out = Exchange("seq", lambda t: csend.at[t], lambda s: cland.at[s], c_send, c_recv)
     span_rows = kvland.shape[0] // KEY_GROUPS
     wide_lane = lax.broadcasted_iota(jnp.int32, (span_rows, 128), 1)
@@ -538,12 +544,11 @@
 
     def attend(part, last):
         span = slice(part * span_rows, (part + 1) * span_rows)
-        per = span_rows // tok
         kv_out.arrived(max(1, part * per), (part + 1) * per)
         vland[span, :] = jnp.where(is_key, jnp.ones((), BF16), kvland[span, :])
 
         def step(d, carry):
-            g = lax.rem(seq // group + d, n_seq // group)
+            g = lax.rem(seq // group + d + 1, n_seq // group)
             tiles = [rows_at(2 * g + i, pair_rows) for i in range(2)]
             both = [
                 lax.dot_general(
@@ -597,6 +602,7 @@
         out_ref[q_half:, p * 128 : (p + 1) * 128] = pltpu.roll(
             jnp.where(lane < 64, two, one), 64, 1
         ).astype(BF16)
+    kv_out.loop(kv_out.send_one, per, n_seq)
     for transfer in started:
         transfer.wait_send()
 

time: 113 us -> 111 us (0.982)
  Pallas kernels: 108 us -> 105 us
    pallas_call x1, Pallas kernels: 108 us -> 105 us  [per_device(): pl.pallas_call(layer_kernel, out_shape=(jax.ShapeDtypeStruct((tok_rows, w...]
where the time goes in v6:
time: 111 us; the launch traced here: 109 us
  Pallas kernels  105 us (95%)
  local copies, waits for them, and re-layouts  3.54 us (3%)
    pallas_call x1, Pallas kernels, per_device(): pl.pallas_call(layer_kernel, out_shape=(jax.ShapeDtypeStruct((tok_rows, w...  105 us
    unnamed x2, local copies, waits for them, and re-layouts  3.54 us

profile of v6, /device:TPU:2, one launch (start us, length us, event | category | flops | bytes accessed | tf_op | source)
XLA Modules:
  0.0 109.4 jit_solution(8723947600965128434)
XLA Ops:
  0.6 105.2 %layer.1 = (bf16[256,1024]{1,0:T(8,128)(2,1)}, bf16[128,1024]{1,0:T(8,128)(2,1)}) custom-call(bf16[256,1024]{1,0:T(8,128)(2,1)} %bitcast.9, s32[1,256]{1,0:T(1,128)} %ids_ref.1, s32[1,256]{1,0:T(1,128)} %slots_ref.1, f32[1,256]{1,0:T(1,128)} %gate_ref.1, f32[1,1024]{1,0:T(1,128)} %bitcast.12, bf16[4,176,1024]{2,1,0:T(8,128)(2,1)} %bitcast.7, ...), custom_call_target="tpu_custom_call" | custom-call | tf_op jit(solution)/shard_map/layer/pallas_call | solution.py:636
  105.8 1.9 %copy.15 = bf16[1,256,1024]{2,1,0:T(8,128)(2,1)} copy(bf16[1,256,1024]{2,1,0:T(8,128)(2,1)} %bitcast.8) | data formatting | bytes 1048576
  107.7 1.7 %copy.16 = bf16[1,128,1024]{2,1,0:T(8,128)(2,1)} copy(bf16[1,128,1024]{2,1,0:T(8,128)(2,1)} %bitcast.11) | data formatting | bytes 524288

commit v7 on v6

--- a/solution.py
+++ b/solution.py
@@ -230,11 +230,15 @@
         qsend[2 * p + 1] = jnp.where(lane < 64, turned[:q_half], pair[q_half:]).astype(BF16)
     pl.semaphore_wait(barrier, greeted)
 
-    started = []
-
-    def go(transfer):
+    started, late = [], []
+
+    def go(transfer, group=started):
         transfer.start()
-        started.append(transfer)
+        group.append(transfer)
+
+    def drain(group):
+        for transfer in group:
+            transfer.wait_send()
 
     chunks, back_chunks = z_send.shape[0], b_send.shape[0]
     wide = enc_ref.shape[1] // chunks
@@ -464,7 +468,7 @@
         zback[:, bcols(c)] = jnp.dot(
             inverse, gback[:, bcols(c)], preferred_element_type=F32
         ).astype(BF16)
-        go(b_out(c))
+        go(b_out(c), late)
         bland[rows_at(exp, zrows), bcols(c)] = zback[rows_at(exp, zrows), bcols(c)]
 
     second_layer(0)
@@ -480,9 +484,10 @@
     q_out = Exchange(
         "seq", lambda t: qsend.at[t], lambda s: qland.at[s], q_send, q_recv
     )
-    go(q_out)
+    go(q_out, late)
     qland[seq] = qsend[seq]
 
+    drain(started)
     diagonal = out_row == in_row
     gate = jnp.sum(jnp.where(diagonal, gate_ref[...], 0.0), axis=1, keepdims=True)
     for c in range(back_chunks):
@@ -531,6 +536,7 @@
         qrows[t * q_count : t * q_count + q_half, :] = top[t * q_half : (t + 1) * q_half]
         qrows[t * q_count + q_half : (t + 1) * q_count, :] = bottom[t * q_half : (t + 1) * q_half]
 
+    drain(late)
     kv_out.loop(kv_out.send_one, 1, per)
     kv_out.start(per, n_seq)
     c_out = Exchange("seq", lambda t: csend.at[t], lambda s: cland.at[s], c_send, c_recv)
@@ -545,6 +551,8 @@
     def attend(part, last):
         span = slice(part * span_rows, (part + 1) * span_rows)
         kv_out.arrived(max(1, part * per), (part + 1) * per)
+        if last:
+            kv_out.loop(kv_out.send_one, per, n_seq)
         vland[span, :] = jnp.where(is_key, jnp.ones((), BF16), kvland[span, :])
 
         def step(d, carry):
@@ -589,11 +597,10 @@
 
             return carry
 
-        lax.fori_loop(0, n_seq // group, step, 0)
+        lax.fori_loop(0, n_seq // group, step, 0, unroll=2)
 
     for part in range(KEY_GROUPS):
         attend(part, part == KEY_GROUPS - 1)
-    started.append(c_out)
     cland[seq] = csend[seq]
     c_out.arrived()
     for p in range(HEADS // 2):
@@ -602,9 +609,7 @@
         out_ref[q_half:, p * 128 : (p + 1) * 128] = pltpu.roll(
             jnp.where(lane < 64, two, one), 64, 1
         ).astype(BF16)
-    kv_out.loop(kv_out.send_one, per, n_seq)
-    for transfer in started:
-        transfer.wait_send()
+    c_out.wait_send()
 
 
 def per_device(

time: 111 us -> 110 us (level)
  no operation moved by 1% of the time
where the time goes in v7:
time: 110 us; the launch traced here: 108 us
  Pallas kernels  104 us (95%)
  local copies, waits for them, and re-layouts  3.54 us (3%)
    pallas_call x1, Pallas kernels, per_device(): pl.pallas_call(layer_kernel, out_shape=(jax.ShapeDtypeStruct((tok_rows, w...  104 us
    unnamed x2, local copies, waits for them, and re-layouts  3.54 us

profile of v7, /device:TPU:2, one launch (start us, length us, event | category | flops | bytes accessed | tf_op | source)
XLA Modules:
  0.0 108.3 jit_solution(13308671699731016664)
XLA Ops:
  0.6 104.1 %layer.1 = (bf16[256,1024]{1,0:T(8,128)(2,1)}, bf16[128,1024]{1,0:T(8,128)(2,1)}) custom-call(bf16[256,1024]{1,0:T(8,128)(2,1)} %bitcast.9, s32[1,256]{1,0:T(1,128)} %ids_ref.1, s32[1,256]{1,0:T(1,128)} %slots_ref.1, f32[1,256]{1,0:T(1,128)} %gate_ref.1, f32[1,1024]{1,0:T(1,128)} %bitcast.12, bf16[4,176,1024]{2,1,0:T(8,128)(2,1)} %bitcast.7, ...), custom_call_target="tpu_custom_call" | custom-call | tf_op jit(solution)/shard_map/layer/pallas_call | solution.py:641
  104.7 1.9 %copy.15 = bf16[1,256,1024]{2,1,0:T(8,128)(2,1)} copy(bf16[1,256,1024]{2,1,0:T(8,128)(2,1)} %bitcast.8) | data formatting | bytes 1048576
  106.6 1.7 %copy.16 = bf16[1,128,1024]{2,1,0:T(8,128)(2,1)} copy(bf16[1,128,1024]{2,1,0:T(8,128)(2,1)} %bitcast.11) | data formatting | bytes 524288

commit v8 on v7

--- a/solution.py
+++ b/solution.py
@@ -76,7 +76,15 @@
         lax.fori_loop(first, self.n if last is None else last, body, 0)
 
     def start(self, first=1, last=None):
-        self.loop(self.start_one, first, last)
+        if self.route:
+            self.loop(self.start_one, first, last)
+            return
+
+        def outward(i):
+            side = 2 * lax.rem(i, 2) - 1
+            self.start_one(self.n // 2 + side * ((i + 1) // 2))
+
+        self.loop(outward, 0, self.n - 1)
 
     def arrived(self, first=1, last=None):
         self.loop(self.wait_one, first, last)

time: 110 us -> 109 us (level)
    pallas_call x1, Pallas kernels: 104 us -> 103 us  [per_device(): pl.pallas_call(layer_kernel, out_shape=(jax.ShapeDtypeStruct((tok_rows, w...]
where the time goes in v8:
time: 109 us; the launch traced here: 107 us
  Pallas kernels  103 us (94%)
  local copies, waits for them, and re-layouts  3.54 us (3%)
    pallas_call x1, Pallas kernels, per_device(): pl.pallas_call(layer_kernel, out_shape=(jax.ShapeDtypeStruct((tok_rows, w...  103 us
    unnamed x2, local copies, waits for them, and re-layouts  3.54 us

profile of v8, /device:TPU:2, one launch (start us, length us, event | category | flops | bytes accessed | tf_op | source)
XLA Modules:
  0.0 106.9 jit_solution(9097561229110312911)
XLA Ops:
  0.6 102.7 %layer.1 = (bf16[256,1024]{1,0:T(8,128)(2,1)}, bf16[128,1024]{1,0:T(8,128)(2,1)}) custom-call(bf16[256,1024]{1,0:T(8,128)(2,1)} %bitcast.9, s32[1,256]{1,0:T(1,128)} %ids_ref.1, s32[1,256]{1,0:T(1,128)} %slots_ref.1, f32[1,256]{1,0:T(1,128)} %gate_ref.1, f32[1,1024]{1,0:T(1,128)} %bitcast.12, bf16[4,176,1024]{2,1,0:T(8,128)(2,1)} %bitcast.7, ...), custom_call_target="tpu_custom_call" | custom-call | tf_op jit(solution)/shard_map/layer/pallas_call | solution.py:649
  103.3 1.9 %copy.15 = bf16[1,256,1024]{2,1,0:T(8,128)(2,1)} copy(bf16[1,256,1024]{2,1,0:T(8,128)(2,1)} %bitcast.8) | data formatting | bytes 1048576
  105.2 1.7 %copy.16 = bf16[1,128,1024]{2,1,0:T(8,128)(2,1)} copy(bf16[1,128,1024]{2,1,0:T(8,128)(2,1)} %bitcast.11) | data formatting | bytes 524288
